TPU v7x, 256 devices: a whole 4x4x8 slice. The times are simulated.
256 devices in a mesh: seq: 32 (over x, y, core), head: 8 (over z).
Axes of the slice: x: 4, y: 4, z: 8, core: 2. Of those that a mesh axis runs over, the one named last changes fastest.
Arguments:
- hidden_in: bfloat16 [16384, 2048], P('seq', 'head'), may hold values from -8 to 8
- proj_weight: bfloat16 [2048, 10240], P(None, 'head'), may hold values from -0.125 to 0.125
- beta_weight: bfloat16 [2048, 32], P(None, 'head'), may hold values from -1 to 1
- norm_gain: float32 [2048], P('head'), may hold values from 0.1 to 1.9
- out_weight: bfloat16 [2048, 2048], P('head'), may hold values from -0.125 to 0.125
- cotangent: bfloat16 [16384, 2048], P('seq', 'head'), may hold values from -6 to 6
Outputs:
- mixed_out: bfloat16 [16384, 2048], P('seq', 'head')
- grad_input: bfloat16 [16384, 2048], P('seq', 'head')
All inputs are finite; a program needn't handle non-finite values.
Results may differ from a plain program's by a relative error of at most 0.02.
Values may be sent and summed in bfloat16 or wider, within the bound.
A program may use at most 128 MiB of HBM per device.

v0:
```python
from functools import partial

import jax
import jax.numpy as jnp
from jax import lax
from jax.sharding import PartitionSpec as P

DK = 128
REFL = 2


HIGHEST = lax.Precision.HIGHEST


def passed_along(shard, axis, by):
    size = lax.axis_size(axis)
    pairs = [(i, i + by) for i in range(size) if 0 <= i + by < size]
    return lax.ppermute(shard, axis, pairs)


def product(left, right):
    return jnp.matmul(left, right, precision=HIGHEST)


def unit_rows(vectors):
    return vectors / jnp.sqrt(jnp.sum(vectors * vectors, axis=-1, keepdims=True) + 1e-06)


def solve_lower(matrix, target):
    return jax.scipy.linalg.solve_triangular(matrix, target, lower=True, unit_diagonal=True)


def prepare_head(projected, beta_logits, block_size):
    row_count = projected.shape[0]
    key_width = projected.shape[1] // (1 + 2 * REFL)
    blocks = row_count // block_size
    pair_span = block_size * REFL
    pieces = projected.reshape(row_count, 1 + 2 * REFL, key_width)
    queries = unit_rows(pieces[:, 0]).reshape(blocks, block_size, key_width)
    key_rows = unit_rows(pieces[:, 1 : 1 + REFL]).reshape(blocks, pair_span, key_width)
    values = pieces[:, 1 + REFL :].reshape(blocks, pair_span, key_width)
    strength = (2.0 * jax.nn.sigmoid(beta_logits)).reshape(blocks, pair_span, 1)
    strict_below = jnp.arange(pair_span)[:, None] > jnp.arange(pair_span)[None, :]
    key_gram = strength * product(key_rows, jnp.swapaxes(key_rows, 1, 2))
    lower_unit = jnp.where(strict_below, key_gram, 0.0) + jnp.eye(pair_span, dtype=jnp.float32)
    target = strength * jnp.concatenate([values, key_rows], axis=2)
    solved = jax.vmap(solve_lower)(lower_unit, target)
    return (queries, key_rows, solved[:, :, key_width:], solved[:, :, :key_width])


def compose_head(key_rows, shifts, updates):
    key_width = key_rows.shape[2]
    identity = jnp.eye(key_width, dtype=jnp.float32)
    trans_all = identity - product(jnp.swapaxes(key_rows, 1, 2), shifts)
    writes = product(jnp.swapaxes(key_rows, 1, 2), updates)

    def absorb(state_pair, block_pair):
        return (
            (
                product(block_pair[0], state_pair[0]),
                product(block_pair[0], state_pair[1]) + block_pair[1],
            ),
            None,
        )

    result, _ = lax.scan(absorb, (identity, jnp.zeros_like(identity)), (trans_all, writes))
    return result


def read_head(queries, key_rows, shifts, updates, start_state, gain_row):
    block_size = queries.shape[1]
    pair_span = key_rows.shape[1]
    visible = jnp.arange(pair_span)[None, :] <= REFL * jnp.arange(block_size)[:, None] + REFL - 1

    def advance(memory, block_items):
        query_blk, key_blk, shift_blk, update_blk = block_items
        corrected = update_blk - product(shift_blk, memory)
        scores = jnp.where(visible, product(query_blk, key_blk.T), 0.0)
        output = product(query_blk, memory) + product(scores, corrected)
        return (memory + product(key_blk.T, corrected), output)

    _, outputs = lax.scan(advance, start_state, (queries, key_rows, shifts, updates))
    outputs = outputs.reshape(-1, outputs.shape[2])
    inverse_rms = lax.rsqrt(jnp.mean(outputs * outputs, axis=-1, keepdims=True) + 1e-05)
    return outputs * inverse_rms * gain_row


def local(hidden_in, proj_weight, beta_weight, norm_gain, out_weight, cotangent):
    row_count = hidden_in.shape[0]
    block_size = min(64, row_count)
    head_count = norm_gain.shape[0] // DK
    head_width = proj_weight.shape[1] // head_count
    contract = (((1,), (1,)), ((), ()))
    hidden_part = lax.all_gather(hidden_in, "head", axis=1, tiled=True)
    cot_part = lax.all_gather(cotangent, "head", axis=1, tiled=True)
    projected = jnp.dot(hidden_part, proj_weight, preferred_element_type=jnp.float32)
    beta_logits = jnp.dot(hidden_part, beta_weight, preferred_element_type=jnp.float32)
    dnormed = lax.dot_general(cot_part, out_weight, contract, preferred_element_type=jnp.float32)
    projected, beta_logits, dnormed = (projected, beta_logits, dnormed)
    proj_heads = jnp.moveaxis(projected.reshape(row_count, head_count, head_width), 1, 0)
    logit_heads = jnp.moveaxis(beta_logits.reshape(row_count, head_count, REFL), 1, 0)
    gain_heads = norm_gain.reshape(head_count, DK)
    prepared, prep_pull = jax.vjp(
        jax.vmap(partial(prepare_head, block_size=block_size)), proj_heads, logit_heads
    )
    (transit, offset), compose_pull = jax.vjp(
        jax.vmap(compose_head), prepared[1], prepared[2], prepared[3]
    )
    turn_count = lax.axis_size("seq") - 1

    def forward_turn(turn_index, state_pair):
        incoming = passed_along(state_pair[1], "seq", 1)
        return (incoming, product(transit, incoming) + offset)

    start_state, _ = lax.fori_loop(0, turn_count, forward_turn, (jnp.zeros_like(offset), offset))

    def read_all(queries, key_rows, shifts, updates, memory):
        return jax.vmap(read_head)(queries, key_rows, shifts, updates, memory, gain_heads)

    normed, read_pull = jax.vjp(
        read_all, prepared[0], prepared[1], prepared[2], prepared[3], start_state
    )
    normed_rows = (
        jnp.moveaxis(normed, 0, 1).reshape(row_count, head_count * DK).astype(jnp.bfloat16)
    )
    mixed_terms = jnp.dot(normed_rows, out_weight, preferred_element_type=jnp.float32)
    mixed_out = lax.psum_scatter(
        mixed_terms.astype(jnp.bfloat16), "head", scatter_dimension=1, tiled=True
    )
    dnormed_heads = jnp.moveaxis(dnormed.reshape(row_count, head_count, DK), 1, 0)
    grad_query, grad_keys, grad_shifts, grad_updates, grad_start = read_pull(dnormed_heads)
    transit_back = jnp.swapaxes(transit, 1, 2)

    def backward_turn(turn_index, state_pair):
        arriving = passed_along(state_pair[1], "seq", -1)
        return (arriving, grad_start + product(transit_back, arriving))

    after_grad, _ = lax.fori_loop(
        0, turn_count, backward_turn, (jnp.zeros_like(grad_start), grad_start)
    )
    keys_extra, shifts_extra, updates_extra = compose_pull(
        (product(after_grad, jnp.swapaxes(start_state, 1, 2)), after_grad)
    )
    grad_proj, grad_logit = prep_pull(
        (
            grad_query,
            grad_keys + keys_extra,
            grad_shifts + shifts_extra,
            grad_updates + updates_extra,
        )
    )
    proj_back = (
        jnp.moveaxis(grad_proj, 0, 1)
        .reshape(row_count, head_count * head_width)
        .astype(jnp.bfloat16)
    )
    logit_back = (
        jnp.moveaxis(grad_logit, 0, 1).reshape(row_count, head_count * REFL).astype(jnp.bfloat16)
    )
    input_term = lax.dot_general(
        proj_back, proj_weight, contract, preferred_element_type=jnp.float32
    )
    input_term = input_term + lax.dot_general(
        logit_back, beta_weight, contract, preferred_element_type=jnp.float32
    )
    grad_input = lax.psum_scatter(
        input_term.astype(jnp.bfloat16), "head", scatter_dimension=1, tiled=True
    )
    return (mixed_out, grad_input)


def solution(mesh):
    placed = (
        P("seq", "head"),
        P(None, "head"),
        P(None, "head"),
        P("head"),
        P("head", None),
        P("seq", "head"),
    )
    return jax.shard_map(
        local,
        mesh=mesh,
        in_specs=placed,
        out_specs=(P("seq", "head"), P("seq", "head")),
        check_vma=False,
    )
```

profile of v0, /device:TPU:64, one launch (start us, length us, event | category | flops | bytes accessed | tf_op | source)
XLA Modules:
  0.0 1185.7 jit_solution(16306266539693993664)
XLA Ops:
  9.6 48.5 %all-gather.3.cloned.1.call-done = bf16[512,2048]{1,0:T(8,128)(2,1)} async-done(((bf16[512,256]{1,0:T(8,128)(2,1)}), bf16[512,2048]{1,0:T(8,128)(2,1)}) %all-gather.3.cloned.1.call-update) | async-done | bytes 2097168 | tf_op jit(solution)/shard_map/all_gather | solution.py:94
  58.1 5.5 fusion.148
  79.5 158.8 %custom-call.10 = f32[2,8,1,128,128]{3,4,2,1,0:T(8,128)} custom-call(f32[2,8,1,128,128]{4,3,2,1,0:T(8,128)} %add_bitcast_fusion), custom_call_target="InvertDiagBlocksLowerTriangular" | custom-call | tf_op jit(solution)/shard_map/jvp(vmap(vmap(jit(_solve_triangular))))/triangular_solve | solution.py:30
  253.8 25.7 %while.113 = (s32[]{:T(128)}, f32[2,128,128]{2,1,0:T(8,128)S(1)}, f32[2,128,128]{2,1,0:T(8,128)S(1)}, f32[8,2,128,128]{3,2,1,0:T(8,128)}, f32[8,2,128,128]{3,2,1...) while((s32[]{:T(128)}, f32[2,128,128]{2,1,0:T(8,128)S(1)}, ...), condition=%wide.region_2.3_spmd.clone, body=%wide.region_1.0_spmd.clone.sunk | while | flops 100761600 | bytes 1967735 | solution.py:66
  280.1 246.0 %while.109 = (s32[]{:T(128)}, f32[2,128,128]{2,1,0:T(8,128)}, f32[2,128,128]{2,1,0:T(8,128)S(1)}, f32[2,128,128]{2,1,0:T(8,128)S(1)}, f32[2,128,128]{2,1,0:T(8,128)S(1)}, /*index=5*/s32[]{:T(128)}) while((s32[]{:T(128)}, f32[2,128,128]{2,1,0:T(8,128)}, f32[2,128,128]{2,1,0:T(8,128)S(1)}, f32[2,128,128]{2,1,0:T(8,128)S(1)}, ...), condition=%wide.region_4.5_spmd, body=%wide.region_3.4_spmd.sunk | while | flops 50364416 | bytes 1573001 | solution.py:115
  289.7 5.3 collective-permute-start
  296.7 5.3 collective-permute-start
  303.6 5.3 collective-permute-start
  317.4 5.3 collective-permute-start
  324.4 5.3 collective-permute-start
  372.9 6.9 collective-permute-start
  381.4 7.4 collective-permute-start
  390.5 7.4 collective-permute-start
  399.5 7.4 collective-permute-start
  408.6 7.4 collective-permute-start
  417.6 7.4 collective-permute-start
  426.7 7.4 collective-permute-start
  435.7 7.4 collective-permute-start
  444.7 7.4 collective-permute-start
  453.8 7.4 collective-permute-start
  462.8 7.4 collective-permute-start
  471.9 7.4 collective-permute-start
  480.9 7.4 collective-permute-start
  489.9 7.4 collective-permute-start
  499.0 7.4 collective-permute-start
  508.0 7.4 collective-permute-start
  517.1 7.4 collective-permute-start
  534.1 50.5 %while.112 = (s32[]{:T(128)}, f32[2,128,128]{2,1,0:T(8,128)S(1)}, f32[8,2,64,128]{3,2,0,1:T(8,128)S(1)}, f32[8,2,128,128]{3,2,1,0:T(8,128)}, f32[8,2,128,128]{3,...) while((s32[]{:T(128)}, f32[2,128,128]{2,1,0:T(8,128)S(1)}, ...), condition=%wide.region_7.8_spmd.clone, body=%wide.region_6.7_spmd.clone.sunk | while | flops 176259072 | bytes 3156117 | solution.py:82
  597.2 117.7 %while.114 = (s32[]{:T(128)}, f32[2,128,128]{2,1,0:T(8,128)S(1)}, f32[8,2,64,128]{3,2,0,1:T(8,128)S(1)}, f32[8,2,128,128]{3,2,0,1:T(8,128)}, f32[8,2,128,128]{3,...) while((s32[]{:T(128)}, f32[2,128,128]{2,1,0:T(8,128)S(1)}, ...), condition=%wide.region_12.13_spmd.clone, body=%wide.region_11.12_spmd.clone.sunk | while | flops 352649216 | bytes 3883208 | solution.py:82
  715.8 282.5 %while.110 = (s32[]{:T(128)}, f32[2,128,128]{2,1,0:T(8,128)}, f32[2,128,128]{2,1,0:T(8,128)S(1)}, f32[2,128,128]{2,1,0:T(8,128)S(1)}, f32[2,128,128]{2,1,0:T(8,128)S(1)}, /*index=5*/s32[]{:T(128)}) while((s32[]{:T(128)}, f32[2,128,128]{2,1,0:T(8,128)}, f32[2,128,128]{2,1,0:T(8,128)S(1)}, f32[2,128,128]{2,1,0:T(8,128)S(1)}, ...), condition=%wide.region_14.15_spmd, body=%wide.region_13.14_spmd.sunk | while | flops 50364416 | bytes 1573001 | solution.py:138
  717.0 7.0 collective-permute-done.1
  726.0 7.8 collective-permute-done.1
  735.7 7.0 collective-permute-done.1
  744.6 7.8 collective-permute-done.1
  754.4 7.0 collective-permute-done.1
  763.3 7.8 collective-permute-done.1
  773.0 7.0 collective-permute-done.1
  781.9 7.8 collective-permute-done.1
  791.7 7.1 collective-permute-done.1
  800.7 7.1 collective-permute-done.1
  809.7 7.1 collective-permute-done.1
  818.8 7.1 collective-permute-done.1
  827.8 7.1 collective-permute-done.1
  836.9 7.1 collective-permute-done.1
  845.9 7.1 collective-permute-done.1
  854.9 7.1 collective-permute-done.1
  864.0 7.1 collective-permute-done.1
  873.0 7.1 collective-permute-done.1
  882.0 7.1 collective-permute-done.1
  891.1 7.1 collective-permute-done.1
  900.1 7.1 collective-permute-done.1
  909.2 7.1 collective-permute-done.1
  918.2 7.1 collective-permute-done.1
  927.2 7.1 collective-permute-done.1
  936.3 7.1 collective-permute-done.1
  945.3 7.1 collective-permute-done.1
  954.3 7.1 collective-permute-done.1
  963.4 7.1 collective-permute-done.1
  972.4 7.1 collective-permute-done.1
  981.5 7.1 collective-permute-done.1
  990.5 7.1 collective-permute-done.1
  1000.8 47.4 %while.111 = (s32[]{:T(128)}, f32[2,128,128]{2,1,0:T(8,128)S(1)}, f32[2,128,128]{2,1,0:T(8,128)S(1)}, f32[8,2,128,128]{2,3,1,0:T(8,128)}, f32[8,2,128,128]{3,2,1...) while((s32[]{:T(128)}, f32[2,128,128]{2,1,0:T(8,128)S(1)}, ...), condition=%wide.region_16.17_spmd, body=%wide.region_15.16_spmd.sunk | while | flops 201359360 | bytes 2491529 | solution.py:66
  1103.9 31.1 %reduce-scatter.3.cloned.1.call-done = bf16[512,256]{1,0:T(8,128)(2,1)} async-done(((bf16[512,2048]{1,0:T(8,128)(2,1)}), bf16[512,256]{1,0:T(8,128)(2,1)}) %reduce-scatter.3.cloned.1.call-update) | async-done | bytes 262160 | tf_op jit(solution)/shard_map/reduce_scatter | solution.py:127
  1135.0 44.0 %reduce-scatter.5.cloned.1.call-done = bf16[512,256]{1,0:T(8,128)(2,1)} async-done(((bf16[512,2048]{1,0:T(8,128)(2,1)}), bf16[512,256]{1,0:T(8,128)(2,1)}) %reduce-scatter.5.cloned.1.call-update) | async-done | bytes 262160 | tf_op jit(solution)/shard_map/reduce_scatter | solution.py:166
  (679 shorter events, 505.9 us)
Async XLA Ops:
  7.2 50.9 %all-gather.3.cloned.1.call-start = ((), (), s32[]{:S(2)}) async-start(), calls=%async_computation.2 | async-start | bytes 2359296 | tf_op jit(solution)/shard_map/all_gather | solution.py:94
  7.9 576.7 %all-gather.5.cloned.1.call-start = ((), (), s32[]{:S(2)}) async-start(), calls=%async_computation.4 | async-start | bytes 2359296 | tf_op jit(solution)/shard_map/all_gather | solution.py:95
  8.7 1126.4 %reduce-scatter.3.cloned.1.call-start = ((), (), s32[]{:S(2)}) async-start(), calls=%async_computation.3 | async-start | bytes 2359296 | tf_op jit(solution)/shard_map/reduce_scatter | solution.py:127
  289.7 6.3 collective-permute-start
  296.7 6.3 collective-permute-start
  303.6 6.3 collective-permute-start
  310.5 6.3 collective-permute-start
  317.4 6.3 collective-permute-start
  324.4 6.3 collective-permute-start
  331.3 6.3 collective-permute-start
  338.2 6.3 collective-permute-start
  345.2 6.3 collective-permute-start
  352.1 6.3 collective-permute-start
  359.0 6.3 collective-permute-start
  366.0 6.3 collective-permute-start
  372.9 7.9 collective-permute-start
  381.4 8.4 collective-permute-start
  390.5 8.4 collective-permute-start
  399.5 8.4 collective-permute-start
  408.6 8.4 collective-permute-start
  417.6 8.4 collective-permute-start
  426.7 8.4 collective-permute-start
  435.7 8.4 collective-permute-start
  444.7 8.4 collective-permute-start
  453.8 8.4 collective-permute-start
  462.8 8.4 collective-permute-start
  471.9 8.4 collective-permute-start
  480.9 8.4 collective-permute-start
  489.9 8.4 collective-permute-start
  499.0 8.4 collective-permute-start
  508.0 8.4 collective-permute-start
  517.1 8.4 collective-permute-start
  715.8 8.3 collective-permute-start.1
  724.7 9.1 collective-permute-start.1
  734.4 8.3 collective-permute-start.1
  743.3 9.1 collective-permute-start.1
  753.1 8.3 collective-permute-start.1
  762.0 9.1 collective-permute-start.1
  771.7 8.3 collective-permute-start.1
  780.6 9.1 collective-permute-start.1
  790.4 8.4 collective-permute-start.1
  799.4 8.4 collective-permute-start.1
  808.4 8.4 collective-permute-start.1
  817.5 8.4 collective-permute-start.1
  826.5 8.4 collective-permute-start.1
  835.6 8.4 collective-permute-start.1
  844.6 8.4 collective-permute-start.1
  853.6 8.4 collective-permute-start.1
  862.7 8.4 collective-permute-start.1
  871.7 8.4 collective-permute-start.1
  880.8 8.4 collective-permute-start.1
  889.8 8.4 collective-permute-start.1
  898.8 8.4 collective-permute-start.1
  907.9 8.4 collective-permute-start.1
  916.9 8.4 collective-permute-start.1
  925.9 8.4 collective-permute-start.1
  935.0 8.4 collective-permute-start.1
  944.0 8.4 collective-permute-start.1
  953.1 8.4 collective-permute-start.1
  962.1 8.4 collective-permute-start.1
  971.1 8.4 collective-permute-start.1
  980.2 8.4 collective-permute-start.1
  989.2 8.4 collective-permute-start.1
  1065.1 113.9 %reduce-scatter.5.cloned.1.call-start = ((), (), s32[]{:S(2)}) async-start(), calls=%async_computation.5 | async-start | bytes 2359296 | tf_op jit(solution)/shard_map/reduce_scatter | solution.py:166
  (106 other events, 1985.5 us)
Sparse Core Ops, SparseCore 0:
  9.7 48.3 all-gather.2
  59.8 47.3 all-gather.4
  1065.2 69.7 reduce-scatter.2
  1138.0 40.9 reduce-scatter.4
where the time goes:
time: 1200 us; the launch traced here: 1190 us
  waiting for transfers between devices  377 us (31%)
  matrix products  306 us (26%)
  starting transfers between devices  236 us (20%)
  other arithmetic  181 us (15%)
  local copies, waits for them, and re-layouts  68.6 us (6%)
  between operations  14.6 us (1%)
    dot_general x240, matrix products, product(): return jnp.matmul(left, right, precision=HIGHEST)  271 us
    ppermute x62, waiting for transfers between devices, passed_along(): return lax.ppermute(shard, axis, pairs)  252 us
    ppermute x62, starting transfers between devices, passed_along(): return lax.ppermute(shard, axis, pairs)  235 us
    another operation x3, other arithmetic, solve_lower(): jax.scipy.linalg.solve_triangular(matrix, target, lower=True, unit_diagon...  161 us
    all_gather x1, waiting for transfers between devices, local(): hidden_part = lax.all_gather(hidden_in, 'head', axis=1, tiled=True)  48.5 us
    reduce_scatter x1, waiting for transfers between devices, local(): lax.psum_scatter(input_term.astype(jnp.bfloat16), 'head', scatter_dimensi...  44 us
    reduce_scatter x1, waiting for transfers between devices, local(): lax.psum_scatter(mixed_terms.astype(jnp.bfloat16), 'head', scatter_dimens...  31.1 us
  transfers between devices with their start and end apart: 66, of which 65 were waited for; matrix products, arithmetic and copies ran while one was open for 27% of the time, Pallas kernels for 0%

commit v1 on v0

v1 whole, which is shorter than its diff:
```python
import jax
import jax.numpy as jnp
from jax import lax
from jax.experimental import pallas as pl
from jax.experimental.pallas import tpu as pltpu
from jax.sharding import PartitionSpec as P

DK = 128
REFL = 2
CT = 64
CR = CT * REFL
MESH = pl.DeviceIdType.MESH
F32 = jnp.float32
BF16 = jnp.bfloat16
VM = pl.BlockSpec(memory_space=pltpu.VMEM)


def split(a):
    hi = a.astype(BF16)
    lo = (a - hi.astype(F32)).astype(BF16)
    return hi, lo


def lhs(a):
    hi, lo = split(a)
    return jnp.concatenate([hi, lo], axis=1)


def rhs(b):
    hi, lo = split(b)
    row = jnp.concatenate([hi, lo], axis=1)
    return jnp.concatenate([row, row], axis=0)


def pmm(a2, b4):
    n = b4.shape[1] // 2
    r = jnp.dot(a2, b4, preferred_element_type=F32)
    return r[:, :n] + r[:, n:]


def mm(a, b):
    return pmm(lhs(a), rhs(b))


def mmt(a, b):
    return pmm(lhs(a.T), rhs(b))


def orders(rows, cols, row_tokens, col_tokens):
    r = lax.broadcasted_iota(jnp.int32, (rows, cols), 0)
    c = lax.broadcasted_iota(jnp.int32, (rows, cols), 1)
    if row_tokens:
        r_at = r
    else:
        r_at = 2 * (r % CT) + r // CT
    c_at = 2 * (c % CT) + c // CT
    return r_at, c_at


def unit_scale(v, eps):
    return lax.rsqrt(jnp.sum(v * v, axis=1, keepdims=True) + eps)


def head_rows(proj_ref, c, h):
    rows = pl.ds(pl.multiple_of(c * CT, CT), CT)
    base = h * 5 * DK
    return [proj_ref[rows, base + i * DK : base + (i + 1) * DK] for i in range(5)]


def strengths(logit_ref, c, h):
    rows = pl.ds(pl.multiple_of(c * CT, CT), CT)
    x = jnp.concatenate(
        [logit_ref[rows, 2 * h : 2 * h + 1], logit_ref[rows, 2 * h + 1 : 2 * h + 2]], axis=0
    )
    return 1.0 / (1.0 + jnp.exp(-x)), 1.0 / (1.0 + jnp.exp(x))


def crows(c):
    return pl.ds(pl.multiple_of(c * CR, CR), CR)


def trows(c):
    return pl.ds(pl.multiple_of(c * CT, CT), CT)


def place():
    s = lax.axis_index("seq")
    core = lax.rem(s, 2)
    y = lax.rem(lax.div(s, 2), 4)
    x = lax.div(s, 8)
    return x, y, core


def at(x, y, core):
    return (x * 4 + y) * 2 + core


def meet(x, y, core):
    barrier = pltpu.get_barrier_semaphore()
    peers = [at(x, y, 1 - core)]
    for d in (1, 2, 3):
        peers.append(at(x, lax.rem(y + d, 4), core))
        peers.append(at(lax.rem(x + d, 4), y, core))
    for p in peers:
        pl.semaphore_signal(barrier, inc=1, device_id={"seq": p}, device_id_type=MESH)
    pl.semaphore_wait(barrier, len(peers))


def send(src, dst, sems, i, seq):
    return pltpu.make_async_remote_copy(
        src_ref=src,
        dst_ref=dst,
        send_sem=sems.at[0, i],
        recv_sem=sems.at[1, i],
        device_id={"seq": seq},
        device_id_type=MESH,
    )


def compose(later, earlier):
    r = mm(later[:, :DK], earlier)
    return jnp.concatenate([r[:, :DK], r[:, DK:] + later[:, DK:]], axis=1)


def prep_kernel(
    proj, logit,
    q_o, k_o, w_o, uv_o, t_o, a_o, pm_o, po_o, mc_o, start_o, msave_o,
    oc, mo, cslot, yslot, xslot, fin, sems,
):
    heads = 2
    chunks = proj.shape[0] // CT
    x, y, core = place()
    meet(x, y, core)

    def chunk_pair(step, carry):
        r_at, c_at = orders(CR, CR, False, False)
        below = r_at > c_at
        diff = jnp.bitwise_xor(r_at, c_at)
        tr, tc = orders(CT, CR, True, False)
        visible = tc <= 2 * tr + 1
        eye = jnp.where(r_at == c_at, 1.0, 0.0)
        jobs = [(h, 2 * step + cc) for cc in range(2) for h in range(heads)]
        ks, bs, vs, qs = [], [], [], []
        for h, c in jobs:
            a, c1, c2, v1, v2 = head_rows(proj, c, h)
            q = a * unit_scale(a, 1e-6)
            k = jnp.concatenate([c1 * unit_scale(c1, 1e-6), c2 * unit_scale(c2, 1e-6)], axis=0)
            sig, _ = strengths(logit, c, h)
            ks.append(k)
            qs.append(q)
            bs.append(2.0 * sig)
            vs.append(jnp.concatenate([v1, v2], axis=0))
            q_o[h, trows(c), :] = q
            k_o[h, crows(c), :] = k
        kts = [k.T for k in ks]
        kt4 = [rhs(kt) for kt in kts]
        grams = [pmm(lhs(jnp.concatenate([k, q], axis=0)), b4) for k, q, b4 in zip(ks, qs, kt4)]
        for (h, c), g in zip(jobs, grams):
            a_o[h, trows(c), :] = jnp.where(visible, g[CR:], 0.0)
        ns = [jnp.where(below, b * g[:CR], 0.0) for b, g in zip(bs, grams)]
        ts = [eye - jnp.where(diff == 1, n, 0.0) for n in ns]
        level = 1
        while (1 << level) < CR:
            parts = [jnp.where((diff >> level) == 1, n, 0.0) for n in ns]
            inner = [mm(p, t) for p, t in zip(parts, ts)]
            outer = [mm(t, i) for t, i in zip(ts, inner)]
            ts = [t - o for t, o in zip(ts, outer)]
            level += 1
        wus = [mm(t, b * jnp.concatenate([k, v], axis=1)) for t, b, k, v in zip(ts, bs, ks, vs)]
        mos = [pmm(lhs(kt), rhs(wu)) for kt, wu in zip(kts, wus)]
        for (h, c), t, wu, m in zip(jobs, ts, wus, mos):
            t_o[h, crows(c), :] = t
            w_o[h, crows(c), :] = wu[:, :DK]
            uv_o[h, crows(c), :] = wu[:, DK:]
            mc_o[h, crows(c), :] = eye_nat() - m[:, :DK]
            oc[h, crows(c), :] = m[:, DK:]
        return carry

    lax.fori_loop(0, chunks // 2, chunk_pair, 0)

    for h in range(heads):
        mo[h, :, :DK] = eye_nat()
        mo[h, :, DK:] = jnp.zeros((DK, DK), F32)

    def prefix(c, carry):
        for h in range(heads):
            cur = mo[h]
            pm_o[h, crows(c), :] = cur[:, :DK]
            po_o[h, crows(c), :] = cur[:, DK:]
            r = mm(mc_o[h, crows(c), :], cur)
            mo[h, :, :DK] = r[:, :DK]
            mo[h, :, DK:] = r[:, DK:] + oc[h, crows(c), :]
        return carry

    lax.fori_loop(0, chunks, prefix, 0)

    c0 = send(mo.at[1 - core], cslot.at[core], sems, 0, at(x, y, 1 - core))
    c0.start()
    cslot[core] = mo[core]
    c0.wait()
    first = cslot[0]
    chip = compose(cslot[1], first)
    yslot[0] = chip
    sends = [
        send(yslot.at[0], yslot.at[d], sems, d, at(x, lax.rem(y + d, 4), core)) for d in (1, 2, 3)
    ]
    for c in sends:
        c.start()
    for c in sends:
        c.wait()
    got = [yslot[lax.rem(y + 4 - i, 4)] for i in range(4)]
    p1 = got[0]
    p2 = compose(got[1], p1)
    p3 = compose(got[2], p2)
    total = compose(got[3], p3)
    xslot[0] = total
    sends = [
        send(xslot.at[0], xslot.at[d], sems, 3 + d, at(lax.rem(x + d, 4), y, core))
        for d in (1, 2, 3)
    ]
    for c in sends:
        c.start()
    before = jnp.where(y == 1, p1, jnp.where(y == 2, p2, p3))
    for i in range(2):
        msave_o[i] = cslot[i, :, :DK]
    for i in range(4):
        msave_o[2 + i] = got[i][:, :DK]
    for c in sends:
        c.wait()
    gx = [xslot[lax.rem(x + 4 - i, 4)] for i in range(4)]
    for i in range(4):
        msave_o[6 + i] = gx[i][:, :DK]
    s1 = gx[0][:, DK:]
    s2 = mm(gx[1][:, :DK], s1) + gx[1][:, DK:]
    s3 = mm(gx[2][:, :DK], s2) + gx[2][:, DK:]
    group = jnp.where(x == 0, 0.0, jnp.where(x == 1, s1, jnp.where(x == 2, s2, s3)))
    s_chip = jnp.where(y == 0, group, mm(before[:, :DK], group) + before[:, DK:])
    s_next = mm(first[:, :DK], s_chip) + first[:, DK:]
    fin[2] = jnp.where(core == 0, s_next, s_chip)
    c1 = send(fin.at[2], fin.at[core], sems, 7, at(x, y, 1 - core))
    c1.start()
    fin[core] = jnp.where(core == 0, s_chip, s_next)
    c1.wait()
    start_o[0] = fin[0]
    start_o[1] = fin[1]


def eye_nat():
    r = lax.broadcasted_iota(jnp.int32, (DK, DK), 0)
    c = lax.broadcasted_iota(jnp.int32, (DK, DK), 1)
    return jnp.where(r == c, 1.0, 0.0)


def read_kernel(
    proj, logit, gain, dn, q_i, k_i, w_i, uv_i, t_i, a_i, pm_i, po_i, mc_i, start_i, msave_i,
    normed_o, gproj_o, glogit_o,
    s_s, u_s, do_s, y_s, e_s, d_s, esum, ec, yslot, xslot, fin, sems,
):
    heads = 2
    chunks = proj.shape[0] // CT
    x, y, core = place()
    meet(x, y, core)
    for h in range(heads):
        esum[h] = jnp.zeros((DK, DK), F32)

    def forward(step, carry):
        jobs = [(h, 2 * step + cc) for cc in range(2) for h in range(heads)]
        starts = [rhs(start_i[h]) for h in range(heads)]
        states = [
            pmm(lhs(pm_i[h, crows(c), :]), starts[h]) + po_i[h, crows(c), :] for h, c in jobs
        ]
        s4 = [rhs(s) for s in states]
        wq = [
            pmm(lhs(jnp.concatenate([w_i[h, crows(c), :], q_i[h, trows(c), :]], axis=0)), b)
            for (h, c), b in zip(jobs, s4)
        ]
        us = [uv_i[h, crows(c), :] - r[:CR] for (h, c), r in zip(jobs, wq)]
        outs = [r[CR:] + mm(a_i[h, trows(c), :], u) for (h, c), r, u in zip(jobs, wq, us)]
        dos = []
        for (h, c), s, u, o in zip(jobs, states, us, outs):
            g = gain[h : h + 1, :]
            r = lax.rsqrt(jnp.mean(o * o, axis=1, keepdims=True) + 1e-5)
            normed_o[trows(c), h * DK : (h + 1) * DK] = (o * r * g).astype(BF16)
            dy = dn[trows(c), h * DK : (h + 1) * DK] * g
            back = jnp.mean(o * dy, axis=1, keepdims=True)
            do = r * (dy - o * (r * r * back))
            dos.append(do)
            s_s[h, crows(c), :] = s
            u_s[h, crows(c), :] = u
            do_s[h, trows(c), :] = do
        ys = [mmt(a_i[h, trows(c), :], do) for (h, c), do in zip(jobs, dos)]
        es = [
            mmt(q_i[h, trows(c), :], do) - mmt(w_i[h, crows(c), :], yy)
            for (h, c), do, yy in zip(jobs, dos, ys)
        ]
        adds = [mmt(pm_i[h, crows(c), :], e) for (h, c), e in zip(jobs, es)]
        for (h, c), yy, e, add in zip(jobs, ys, es, adds):
            y_s[h, crows(c), :] = yy
            e_s[h, crows(c), :] = e
            esum[h] += add
        return carry

    lax.fori_loop(0, chunks // 2, forward, 0)

    c0 = send(esum.at[1 - core], ec.at[core], sems, 0, at(x, y, 1 - core))
    c0.start()
    ec[core] = esum[core]
    c0.wait()
    e1 = ec[1]
    yslot[0] = mmt(msave_i[0], e1) + ec[0]
    sends = [
        send(yslot.at[0], yslot.at[d], sems, d, at(x, lax.rem(y + d, 4), core)) for d in (1, 2, 3)
    ]
    for c in sends:
        c.start()
    my = [msave_i[2 + i] for i in range(4)]
    suf1 = mm(my[3], my[2])
    suf0 = mm(suf1, my[1])
    suf = jnp.where(y == 2, my[3], jnp.where(y == 1, suf1, suf0))
    for c in sends:
        c.wait()
    got = [yslot[lax.rem(y + 4 - i, 4)] for i in range(4)]
    r3 = got[3]
    r2 = mmt(my[2], r3) + got[2]
    r1 = mmt(my[1], r2) + got[1]
    xslot[0] = mmt(my[0], r1) + got[0]
    sends = [
        send(xslot.at[0], xslot.at[d], sems, 3 + d, at(lax.rem(x + d, 4), y, core))
        for d in (1, 2, 3)
    ]
    for c in sends:
        c.start()
    inside = jnp.where(y == 2, r3, jnp.where(y == 1, r2, r1))
    for c in sends:
        c.wait()
    gx = [xslot[lax.rem(x + 4 - i, 4)] for i in range(4)]
    x2 = gx[3]
    x1 = mmt(msave_i[8], x2) + gx[2]
    x0 = mmt(msave_i[7], x1) + gx[1]
    group = jnp.where(x == 3, 0.0, jnp.where(x == 2, x2, jnp.where(x == 1, x1, x0)))
    d_chip = jnp.where(y == 3, group, mmt(suf, group) + inside)
    d_prev = mmt(msave_i[1], d_chip) + e1
    fin[2] = jnp.where(core == 1, d_prev, d_chip)
    c1 = send(fin.at[2], fin.at[core], sems, 7, at(x, y, 1 - core))
    c1.start()
    fin[core] = jnp.where(core == 1, d_chip, d_prev)
    c1.wait()

    def chain(step, carry):
        c = chunks - 1 - step
        for h in range(heads):
            cur = fin[h]
            d_s[h, crows(c), :] = cur
            fin[h] = mmt(mc_i[h, crows(c), :], cur) + e_s[h, crows(c), :]
        return carry

    lax.fori_loop(0, chunks, chain, 0)

    def backward(step, carry):
        r_at, c_at = orders(CR, CR, False, False)
        below = r_at > c_at
        tr, tc = orders(CT, CR, True, False)
        visible = tc <= 2 * tr + 1
        jobs = [(h, 2 * step + cc) for cc in range(2) for h in range(heads)]
        ks = [k_i[h, crows(c), :] for h, c in jobs]
        k4 = [rhs(k) for k in ks]
        ds = [d_s[h, crows(c), :] for h, c in jobs]
        us = [u_s[h, crows(c), :] for h, c in jobs]
        dus = [mm(k, d) + y_s[h, crows(c), :] for (h, c), k, d in zip(jobs, ks, ds)]
        zs = [mmt(t_i[h, crows(c), :], du) for (h, c), du in zip(jobs, dus)]
        sigs = [strengths(logit, c, h) for h, c in jobs]
        bzs = [2.0 * sg[0] * z for sg, z in zip(sigs, zs)]
        dos = [do_s[h, trows(c), :] for h, c in jobs]
        both = [lhs(jnp.concatenate([bz, do], axis=0)) for bz, do in zip(bzs, dos)]
        pus = [pmm(b2, rhs(u.T)) for b2, u in zip(both, us)]
        pss = [pmm(b2, rhs(s_s[h, crows(c), :].T)) for (h, c), b2 in zip(jobs, both)]
        pbs = [jnp.where(below, p[:CR], 0.0) for p in pus]
        das = [jnp.where(visible, p[CR:], 0.0) for p in pus]
        mixes = [
            pmm(lhs(jnp.concatenate([pb + pb.T, da], axis=0)), kk)
            for pb, da, kk in zip(pbs, das, k4)
        ]
        dks = [
            mm(u, d.T) - ps[:CR] - mx[:CR] + mmt(da, q_i[h, trows(c), :])
            for (h, c), u, d, ps, mx, da in zip(jobs, us, ds, pss, mixes, das)
        ]
        dqs = [mx[CR:] + ps[CR:] for mx, ps in zip(mixes, pss)]
        for (h, c), k, u, z, bz, sg, dk, dq in zip(jobs, ks, us, zs, bzs, sigs, dks, dqs):
            a, c1, c2, _, _ = head_rows(proj, c, h)
            q = q_i[h, trows(c), :]
            sa = unit_scale(a, 1e-6)
            sc = jnp.concatenate([unit_scale(c1, 1e-6), unit_scale(c2, 1e-6)], axis=0)
            ga = sa * (dq - q * jnp.sum(q * dq, axis=1, keepdims=True))
            gc = sc * (dk - k * jnp.sum(k * dk, axis=1, keepdims=True))
            base = h * 5 * DK
            gproj_o[trows(c), base : base + DK] = ga.astype(BF16)
            gproj_o[trows(c), base + DK : base + 2 * DK] = gc[:CT].astype(BF16)
            gproj_o[trows(c), base + 2 * DK : base + 3 * DK] = gc[CT:].astype(BF16)
            gproj_o[trows(c), base + 3 * DK : base + 4 * DK] = bz[:CT].astype(BF16)
            gproj_o[trows(c), base + 4 * DK : base + 5 * DK] = bz[CT:].astype(BF16)
            gl = jnp.sum(z * u, axis=1, keepdims=True) * sg[1]
            glogit_o[trows(c), 2 * h : 2 * h + 1] = gl[:CT].astype(BF16)
            glogit_o[trows(c), 2 * h + 1 : 2 * h + 2] = gl[CT:].astype(BF16)
        return carry

    lax.fori_loop(0, chunks // 2, backward, 0)


def params(collective_id, mib):
    return pltpu.CompilerParams(
        collective_id=collective_id, has_side_effects=True, vmem_limit_bytes=mib << 20
    )


def prepare(projected, logits):
    rows = projected.shape[0]
    h2 = lambda r: jax.ShapeDtypeStruct((2, r, DK), F32)
    full = h2(REFL * rows)
    return pl.pallas_call(
        prep_kernel,
        out_shape=[
            h2(rows), full, full, full, full, h2(rows), full, full, full, h2(DK),
            jax.ShapeDtypeStruct((10, DK, DK), F32),
        ],
        in_specs=[VM, VM],
        out_specs=[VM] * 11,
        scratch_shapes=[
            pltpu.VMEM((2, REFL * rows, DK), F32),
            pltpu.VMEM((2, DK, 2 * DK), F32),
            pltpu.VMEM((2, DK, 2 * DK), F32),
            pltpu.VMEM((4, DK, 2 * DK), F32),
            pltpu.VMEM((4, DK, 2 * DK), F32),
            pltpu.VMEM((3, DK, DK), F32),
            pltpu.SemaphoreType.DMA((2, 8)),
        ],
        compiler_params=params(1, 48),
    )(projected, logits)


def read_back(projected, logits, gains, dnormed, prepared):
    rows = projected.shape[0]
    full = pltpu.VMEM((2, REFL * rows, DK), F32)
    part = pltpu.VMEM((2, rows, DK), F32)
    return pl.pallas_call(
        read_kernel,
        out_shape=[
            jax.ShapeDtypeStruct((rows, 2 * DK), BF16),
            jax.ShapeDtypeStruct((rows, 10 * DK), BF16),
            jax.ShapeDtypeStruct((rows, 4), BF16),
        ],
        in_specs=[VM] * (4 + len(prepared)),
        out_specs=[VM] * 3,
        scratch_shapes=[
            full, full, part, full, full, full,
            pltpu.VMEM((2, DK, DK), F32),
            pltpu.VMEM((2, DK, DK), F32),
            pltpu.VMEM((4, DK, DK), F32),
            pltpu.VMEM((4, DK, DK), F32),
            pltpu.VMEM((3, DK, DK), F32),
            pltpu.SemaphoreType.DMA((2, 8)),
        ],
        compiler_params=params(2, 56),
    )(projected, logits, gains, dnormed, *prepared)


def local(hidden_in, proj_weight, beta_weight, norm_gain, out_weight, cotangent):
    contract = (((1,), (1,)), ((), ()))
    hidden_part = lax.all_gather(hidden_in, "head", axis=1, tiled=True)
    projected = jnp.dot(hidden_part, proj_weight, preferred_element_type=F32)
    logits = jnp.dot(hidden_part, beta_weight, preferred_element_type=F32)
    cotangent, projected = lax.optimization_barrier((cotangent, projected))
    cot_part = lax.all_gather(cotangent, "head", axis=1, tiled=True)
    prepared = prepare(projected, logits)
    dnormed = lax.dot_general(cot_part, out_weight, contract, preferred_element_type=F32)
    normed, grad_proj, grad_logit = read_back(
        projected, logits, norm_gain.reshape(2, DK), dnormed, prepared
    )
    mixed_terms = jnp.dot(normed, out_weight, preferred_element_type=F32)
    mixed_out = lax.psum_scatter(
        mixed_terms.astype(BF16), "head", scatter_dimension=1, tiled=True
    )
    input_term = lax.dot_general(grad_proj, proj_weight, contract, preferred_element_type=F32)
    input_term = input_term + lax.dot_general(
        grad_logit, beta_weight, contract, preferred_element_type=F32
    )
    grad_input = lax.psum_scatter(
        input_term.astype(BF16), "head", scatter_dimension=1, tiled=True
    )
    return (mixed_out, grad_input)


def solution(mesh):
    placed = (
        P("seq", "head"),
        P(None, "head"),
        P(None, "head"),
        P("head"),
        P("head", None),
        P("seq", "head"),
    )
    return jax.shard_map(
        local,
        mesh=mesh,
        in_specs=placed,
        out_specs=(P("seq", "head"), P("seq", "head")),
        check_vma=False,
    )
```

time: 1200 us -> 250 us (0.21)
  matrix products: 306 us -> 21.5 us
  waiting for transfers between devices: 377 us -> 127 us
  starting transfers between devices: 236 us -> 0.16 us
  other arithmetic: 181 us -> 0 us
  Pallas kernels: 0 us -> 79.6 us
  local copies, waits for them, and re-layouts: 68.6 us -> 6.02 us
    dot_general x246 -> x6, matrix products: 288 us -> 21.5 us  [the longest x1 7.63 us: local(): projected = jnp.dot(hidden_part, proj_weight, preferred_element_type=F32)]
    ppermute x62 -> x0, waiting for transfers between devices: 252 us -> none  [passed_along(): return lax.ppermute(shard, axis, pairs)]
    ppermute x62 -> x0, starting transfers between devices: 235 us -> none  [passed_along(): return lax.ppermute(shard, axis, pairs)]
    another operation x4 -> x0, other arithmetic: 161 us -> none  [the longest x3 161 us: solve_lower(): jax.scipy.linalg.solve_triangular(matrix, target, lower=True, unit_diagon...]
    pallas_call x0 -> x2, Pallas kernels: none -> 79.6 us  [the longest x1 42.9 us: prepare(): pl.pallas_call(prep_kernel, out_shape=[h2(rows), full, full, full, full,...]
    while x157 -> x0, local copies, waits for them, and re-layouts: 24 us -> none
    another operation x3 -> x0, matrix products: 12 us -> none  [solve_lower(): jax.scipy.linalg.solve_triangular(matrix, target, lower=True, unit_diagon...]
  transfers between devices with their start and end apart: 66 -> 4, of which waited for: 65 -> 3; matrix products, arithmetic and copies ran while one was open for 27% -> 3% of each run, Pallas kernels for 0% -> 17%
where the time goes in v1:
time: 250 us; the launch traced here: 248 us
  waiting for transfers between devices  127 us (51%)
  Pallas kernels  79.6 us (32%)
  matrix products  21.5 us (9%)
  between operations  13.9 us (6%)
  local copies, waits for them, and re-layouts  6.02 us (2%)
    all_gather x1, waiting for transfers between devices, local(): hidden_part = lax.all_gather(hidden_in, 'head', axis=1, tiled=True)  50.1 us
    reduce_scatter x1, waiting for transfers between devices, local(): lax.psum_scatter(input_term.astype(BF16), 'head', scatter_dimension=1, ti...  44 us
    pallas_call x1, Pallas kernels, prepare(): pl.pallas_call(prep_kernel, out_shape=[h2(rows), full, full, full, full,...  42.9 us
    pallas_call x1, Pallas kernels, read_back(): pl.pallas_call(read_kernel, out_shape=[jax.ShapeDtypeStruct((rows, 2 * DK...  36.7 us
    reduce_scatter x1, waiting for transfers between devices, local(): lax.psum_scatter(mixed_terms.astype(BF16), 'head', scatter_dimension=1, t...  31.7 us
    dot_general x1, matrix products, local(): projected = jnp.dot(hidden_part, proj_weight, preferred_element_type=F32)  7.63 us
    unnamed x26, local copies, waits for them, and re-layouts  6.02 us
  transfers between devices with their start and end apart: 4, of which 3 were waited for; matrix products, arithmetic and copies ran while one was open for 3% of the time, Pallas kernels for 17%

profile of v1, /device:TPU:64, one launch (start us, length us, event | category | flops | bytes accessed | tf_op | source)
XLA Modules:
  0.0 247.7 jit_solution(9574739503740864042)
XLA Ops:
  7.2 0.0 copy-start
  7.2 0.0 all-gather.3.cloned.1.call-start
  7.2 0.7 all-gather.3.cloned.1.call-update
  7.9 0.0 copy-start.10
  7.9 0.0 all-gather.5.cloned.1.call-start
  8.0 50.1 %all-gather.3.cloned.1.call-done = bf16[512,2048]{1,0:T(8,128)(2,1)} async-done(((bf16[512,256]{1,0:T(8,128)(2,1)}), bf16[512,2048]{1,0:T(8,128)(2,1)}) %all-gather.3.cloned.1.call-update) | async-done | bytes 2097168 | tf_op jit(solution)/shard_map/all_gather | solution.py:468
  58.1 0.0 copy-start.11
  58.1 7.6 %fusion.proj = f32[512,1280]{1,0:T(8,128)} fusion(bf16[512,2048]{1,0:T(8,128)(2,1)} %all-gather.3.cloned.1.call-done, bf16[2048,1280]{1,0:T(8,128)(2,1)} %param.7), kind=kOutput, calls=%fused_computation.2 | convolution fusion | flops 2684354560 | bytes 9961472 | tf_op jit(solution)/shard_map/dot_general | solution.py:469
  65.7 0.0 all-gather.5.cloned.1.call-update
  65.7 0.0 reduce-scatter.3.cloned.1.call-start
  65.8 0.0 copy-done.10
  65.8 0.0 copy-done.11
  65.8 0.7 fusion.1.logit
  66.5 0.0 copy-start.4
  66.5 42.9 %shard_map.77 = (f32[2,512,128]{2,1,0:T(8,128)S(1)}, f32[2,1024,128]{2,1,0:T(8,128)S(1)}, f32[2,1024,128]{2,1,0:T(8,128)S(1)}, f32[2,1024,128]{2,1,0:T(8,128)S(1...) custom-call(f32[512,1280]{1,0:T(8,128)} %fusion.proj, ...), custom_call_target="tpu_custom_call" | custom-call | tf_op jit(solution)/shard_map/pallas_call | solution.py:419
  109.4 0.0 copy-start.1
  109.5 1.0 copy-done.1
  110.4 0.0 copy-start.2
  110.4 1.0 copy-done.2
  111.4 0.0 copy-start.3
  111.4 1.0 copy-done.3
  112.3 0.0 copy-start.5
  112.3 0.9 copy-done.5
  113.2 0.0 copy-start.6
  113.2 0.8 copy-done.6
  114.0 0.0 copy-start.7
  114.0 0.8 copy-done.7
  114.8 0.0 copy-start.8
  114.8 0.7 copy-done.8
  115.4 0.0 all-gather.5.cloned.1.call-done
  115.4 0.0 copy-done
  115.4 3.2 %fusion.2.dn = f32[512,256]{1,0:T(8,128)} fusion(bf16[512,2048]{1,0:T(8,128)(2,1)} %all-gather.5.cloned.1.call-done, bf16[256,2048]{1,0:T(8,128)(2,1)S(1)} %copy-done), kind=kOutput, calls=%fused_computation.4 | convolution fusion | flops 536870912 | bytes 3670016 | tf_op jit(solution)/shard_map/dot_general | solution.py:474
  118.6 0.0 copy-done.4
  118.6 36.7 %shard_map.78 = (bf16[512,256]{1,0:T(8,128)(2,1)}, bf16[512,1280]{1,0:T(8,128)(2,1)}, bf16[512,4]{1,0:T(8,128)(2,1)}) custom-call(f32[512,1280]{1,0:T(8,128)} %fusion.proj, f32[512,4]{1,0:T(8,128)} %copy-done.4, f32[2,128]{1,0:T(2,128)} %bitcast.13, f32[512,256]{1,0:T(8,128)} %fusion.2.dn, f32[2,512,128]{2,1,0:T(8,128)} %copy-done.6, ...), custom_call_target="tpu_custom_call" | custom-call | tf_op jit(solution)/shard_map/pallas_call | solution.py:444
  155.3 0.0 copy-start.12
  155.3 3.1 %convolution_convert_fusion = bf16[512,2048]{1,0:T(8,128)(2,1)} fusion(bf16[512,256]{1,0:T(8,128)(2,1)} %get-tuple-element.31, bf16[256,2048]{1,0:T(8,128)(2,1)S(1)} %copy-done), kind=kOutput, calls=%fused_computation.1 | convolution fusion | flops 537919488 | bytes 3407872 | tf_op jit(solution)/shard_map/dot_general | solution.py:478
  158.4 0.0 reduce-scatter.3.cloned.1.call-update
  158.4 0.0 reduce-scatter.5.cloned.1.call-start
  158.5 0.0 copy-done.12
  158.5 0.0 copy-start.9
  158.5 4.9 %fusion.3 = f32[512,2048]{1,0:T(8,128)S(1)} fusion(bf16[512,1280]{1,0:T(8,128)(2,1)S(1)} %copy-done.12, bf16[2048,1280]{1,0:T(8,128)(2,1)} %param.7), kind=kOutput, calls=%fused_computation.5 | convolution fusion | flops 2684354560 | bytes 10747904 | tf_op jit(solution)/shard_map/dot_general | solution.py:482
  163.4 0.0 copy-done.9
  163.4 2.0 add_convert_fusion
  165.4 0.0 reduce-scatter.5.cloned.1.call-update
  165.4 31.7 %reduce-scatter.3.cloned.1.call-done = bf16[512,256]{1,0:T(8,128)(2,1)} async-done(((bf16[512,2048]{1,0:T(8,128)(2,1)}), bf16[512,256]{1,0:T(8,128)(2,1)}) %reduce-scatter.3.cloned.1.call-update) | async-done | bytes 262160 | tf_op jit(solution)/shard_map/reduce_scatter | solution.py:479
  197.2 44.0 %reduce-scatter.5.cloned.1.call-done = bf16[512,256]{1,0:T(8,128)(2,1)} async-done(((bf16[512,2048]{1,0:T(8,128)(2,1)}), bf16[512,256]{1,0:T(8,128)(2,1)}) %reduce-scatter.5.cloned.1.call-update) | async-done | bytes 262160 | tf_op jit(solution)/shard_map/reduce_scatter | solution.py:486
Async XLA Ops:
  7.2 108.3 %copy-start = (bf16[256,2048]{1,0:T(8,128)(2,1)S(1)}, bf16[256,2048]{1,0:T(8,128)(2,1)}, u32[]{:S(2)}) copy-start(bf16[256,2048]{1,0:T(8,128)(2,1)} %param.10) | copy-start | bytes 3145732
  7.2 50.9 %all-gather.3.cloned.1.call-start = ((), (), s32[]{:S(2)}) async-start(), calls=%async_computation.2 | async-start | bytes 2359296 | tf_op jit(solution)/shard_map/all_gather | solution.py:468
  7.9 57.9 %copy-start.10 = (bf16[2048,4]{0,1:T(4,128)(2,1)S(1)}, bf16[2048,4]{0,1:T(4,128)(2,1)}, u32[]{:S(2)}) copy-start(bf16[2048,4]{0,1:T(4,128)(2,1)} %param.8) | copy-start | bytes 49156
  7.9 107.5 %all-gather.5.cloned.1.call-start = ((), (), s32[]{:S(2)}) async-start(), calls=%async_computation.3 | async-start | bytes 2359296 | tf_op jit(solution)/shard_map/all_gather | solution.py:472
  58.1 7.7 %copy-start.11 = (bf16[512,2048]{1,0:T(8,128)(2,1)S(1)}, bf16[512,2048]{1,0:T(8,128)(2,1)}, u32[]{:S(2)}) copy-start(bf16[512,2048]{1,0:T(8,128)(2,1)} %all-gather.3.cloned.1.call-done) | copy-start | bytes 6291460
  65.7 131.4 %reduce-scatter.3.cloned.1.call-start = ((), (), s32[]{:S(2)}) async-start(), calls=%async_computation.4 | async-start | bytes 2359296 | tf_op jit(solution)/shard_map/reduce_scatter | solution.py:479
  66.5 52.1 %copy-start.4 = (f32[512,4]{1,0:T(8,128)}, f32[512,4]{1,0:T(8,128)S(1)}, u32[]{:S(2)}) copy-start(f32[512,4]{1,0:T(8,128)S(1)} %fusion.1.logit) | copy-start | bytes 24580
  109.4 1.0 copy-start.1
  110.4 1.0 copy-start.2
  111.4 1.0 copy-start.3
  112.3 0.9 copy-start.5
  113.2 0.8 copy-start.6
  114.0 0.8 copy-start.7
  114.8 0.7 copy-start.8
  155.3 3.2 %copy-start.12 = (bf16[512,1280]{1,0:T(8,128)(2,1)S(1)}, bf16[512,1280]{1,0:T(8,128)(2,1)}, u32[]{:S(2)}) copy-start(bf16[512,1280]{1,0:T(8,128)(2,1)} %get-tuple-element.32) | copy-start | bytes 3932164
  158.4 82.7 %reduce-scatter.5.cloned.1.call-start = ((), (), s32[]{:S(2)}) async-start(), calls=%async_computation.5 | async-start | bytes 2359296 | tf_op jit(solution)/shard_map/reduce_scatter | solution.py:486
  158.5 4.9 %copy-start.9 = (bf16[512,4]{1,0:T(8,128)(2,1)S(1)}, bf16[512,4]{1,0:T(8,128)(2,1)}, u32[]{:S(2)}) copy-start(bf16[512,4]{1,0:T(8,128)(2,1)} %get-tuple-element.33) | copy-start | bytes 12292
Sparse Core Ops, SparseCore 0:
  9.7 48.3 all-gather.2
  65.9 45.9 all-gather.4
  158.6 38.5 reduce-scatter.2
  200.1 40.9 reduce-scatter.4

commit v2 on v1

v2 whole, which is shorter than its diff:
```python
import jax
import jax.numpy as jnp
from jax import lax
from jax.experimental import pallas as pl
from jax.experimental.pallas import tpu as pltpu
from jax.sharding import PartitionSpec as P

DK = 128
REFL = 2
CT = 64
CR = CT * REFL
MESH = pl.DeviceIdType.MESH
F32 = jnp.float32
BF16 = jnp.bfloat16
VM = pl.BlockSpec(memory_space=pltpu.VMEM)


def split(a):
    hi = a.astype(BF16)
    lo = (a - hi.astype(F32)).astype(BF16)
    return hi, lo


def lhs(a):
    hi, lo = split(a)
    return jnp.concatenate([hi, lo], axis=1)


def rhs(b):
    hi, lo = split(b)
    row = jnp.concatenate([hi, lo], axis=1)
    return jnp.concatenate([row, row], axis=0)


def pmm(a2, b4):
    n = b4.shape[1] // 2
    r = jnp.dot(a2, b4, preferred_element_type=F32)
    return r[:, :n] + r[:, n:]


def mm(a, b):
    return pmm(lhs(a), rhs(b))


def mmt(a, b):
    return pmm(lhs(a.T), rhs(b))


def orders(rows, cols, row_tokens, col_tokens):
    r = lax.broadcasted_iota(jnp.int32, (rows, cols), 0)
    c = lax.broadcasted_iota(jnp.int32, (rows, cols), 1)
    if row_tokens:
        r_at = r
    else:
        r_at = 2 * (r % CT) + r // CT
    c_at = 2 * (c % CT) + c // CT
    return r_at, c_at


def unit_scale(v, eps):
    return lax.rsqrt(jnp.sum(v * v, axis=1, keepdims=True) + eps)


def head_rows(proj_ref, c, h):
    rows = pl.ds(pl.multiple_of(c * CT, CT), CT)
    base = h * 5 * DK
    return [proj_ref[rows, base + i * DK : base + (i + 1) * DK] for i in range(5)]


def strengths(logit_ref, c, h):
    rows = pl.ds(pl.multiple_of(c * CT, CT), CT)
    x = jnp.concatenate(
        [logit_ref[rows, 2 * h : 2 * h + 1], logit_ref[rows, 2 * h + 1 : 2 * h + 2]], axis=0
    )
    return 1.0 / (1.0 + jnp.exp(-x)), 1.0 / (1.0 + jnp.exp(x))


def crows(c):
    return pl.ds(pl.multiple_of(c * CR, CR), CR)


def trows(c):
    return pl.ds(pl.multiple_of(c * CT, CT), CT)


def place():
    s = lax.axis_index("seq")
    core = lax.rem(s, 2)
    y = lax.rem(lax.div(s, 2), 4)
    x = lax.div(s, 8)
    return x, y, core


def at(x, y, core):
    return (x * 4 + y) * 2 + core


def meet(x, y, core, z):
    barrier = pltpu.get_barrier_semaphore()
    peers = [{"seq": at(x, y, 1 - core)}]
    for d in (1, 2, 3):
        peers.append({"seq": at(x, lax.rem(y + d, 4), core)})
        peers.append({"seq": at(lax.rem(x + d, 4), y, core)})
    peers.append({"head": lax.rem(z + 1, 8)})
    peers.append({"head": lax.rem(z + 7, 8)})
    for p in peers:
        pl.semaphore_signal(barrier, inc=1, device_id=p, device_id_type=MESH)
    pl.semaphore_wait(barrier, len(peers))


RIGHT, LEFT = 0, 1
HALF = 256


def beside(z, way):
    return {"head": lax.rem(z + (1 if way == RIGHT else 7), 8)}


def gather_unit(buf, sems, z, way, d, j):
    src, dst = (d - 1, d) if way == RIGHT else ((9 - d) % 8, 8 - d)
    rows = pl.ds(j * HALF, HALF)
    return pltpu.make_async_remote_copy(
        src_ref=buf.at[src, rows],
        dst_ref=buf.at[dst, rows],
        send_sem=sems.at[0, way, d - 1, j],
        recv_sem=sems.at[1, way, d - 1, j],
        device_id=beside(z, way),
        device_id_type=MESH,
    )


def gather_has(way, d, j):
    return d < 4 or (d == 4 and j == way)


def gather_start(buf, sems, z):
    for j in (0, 1):
        for way in (RIGHT, LEFT):
            gather_unit(buf, sems, z, way, 1, j).start()


def gather_step(buf, sems, z, d):
    for j in (0, 1):
        for way in (RIGHT, LEFT):
            if gather_has(way, d, j):
                gather_unit(buf, sems, z, way, d, j).wait_recv()
                if gather_has(way, d + 1, j):
                    gather_unit(buf, sems, z, way, d + 1, j).start()


def gather_end(buf, sems, z):
    for d in (1, 2, 3, 4):
        for j in (0, 1):
            for way in (RIGHT, LEFT):
                if gather_has(way, d, j):
                    gather_unit(buf, sems, z, way, d, j).wait_send()


class Scatter:
    def __init__(self, own, out, sent, came, sems, z):
        self.own, self.out, self.sent, self.came, self.sems, self.z = own, out, sent, came, sems, z

    def unit(self, way, s, j):
        rows = pl.ds(j * HALF, HALF)
        return pltpu.make_async_remote_copy(
            src_ref=self.sent.at[way, s, rows],
            dst_ref=self.came.at[way, s, rows],
            send_sem=self.sems.at[0, way, s, j],
            recv_sem=self.sems.at[1, way, s, j],
            device_id=beside(self.z, way),
            device_id_type=MESH,
        )

    def has(self, way, s, j):
        return s > 0 or j == way

    def step(self, way, s, j):
        if not self.has(way, s, j):
            return
        rows = slice(j * HALF, (j + 1) * HALF)
        dest = lax.rem(self.z + ((4 - s) if way == RIGHT else (4 + s)), 8)
        term = self.own(dest, j)
        if s > 0 and self.has(way, s - 1, j):
            self.unit(way, s - 1, j).wait_recv()
            term = term + self.came[way, s - 1, rows].astype(F32)
        self.sent[way, s, rows] = term.astype(BF16)
        self.unit(way, s, j).start()

    def finish(self):
        for j in (0, 1):
            rows = slice(j * HALF, (j + 1) * HALF)
            term = self.own(self.z, j)
            for way in (RIGHT, LEFT):
                self.unit(way, 3, j).wait_recv()
                term = term + self.came[way, 3, rows].astype(F32)
            self.out[rows, :] = term.astype(BF16)
        for way in (RIGHT, LEFT):
            for s in range(4):
                for j in (0, 1):
                    if self.has(way, s, j):
                        self.unit(way, s, j).wait_send()


def send(src, dst, sems, i, seq):
    return pltpu.make_async_remote_copy(
        src_ref=src,
        dst_ref=dst,
        send_sem=sems.at[0, i],
        recv_sem=sems.at[1, i],
        device_id={"seq": seq},
        device_id_type=MESH,
    )


def compose(later, earlier):
    r = mm(later[:, :DK], earlier)
    return jnp.concatenate([r[:, :DK], r[:, DK:] + later[:, DK:]], axis=1)


def eye_nat():
    r = lax.broadcasted_iota(jnp.int32, (DK, DK), 0)
    c = lax.broadcasted_iota(jnp.int32, (DK, DK), 1)
    return jnp.where(r == c, 1.0, 0.0)


CONTRACT = (((1,), (1,)), ((), ()))


def layer_kernel(
    hid, pw, bw, gain, ow, cot,
    mixed_o, grad_o,
    hids, cots, pw_v, ow_v, proj, logit, dn,
    q_i, k_i, w_i, uv_i, t_i, a_i, pm_i, po_i, mc_i, start_i, msave_i,
    oc, mo, cslot, yslot_f, xslot_f, fin_f,
    s_s, u_s, do_s, y_s, e_s, d_s, esum, ec, yslot_b, xslot_b, fin_b,
    normed, gproj, glogit, msent, mcame, gsent, gcame,
    sems_h, sems_c, sems_f, sems_b, sems_m, sems_g, sems_w,
):
    heads = 2
    chunks = proj.shape[0] // CT
    x, y, core = place()
    z = lax.axis_index("head")
    pw_copy = pltpu.make_async_copy(pw, pw_v, sems_w.at[0])
    ow_copy = pltpu.make_async_copy(ow, ow_v, sems_w.at[1])
    pw_copy.start()
    ow_copy.start()
    hids[0] = hid[...]
    cots[0] = cot[...]
    meet(x, y, core, z)

    gather_start(hids, sems_h, z)
    pw_copy.wait()
    for d in range(5):
        if d > 0:
            gather_step(hids, sems_h, z, d)
        if d == 3:
            gather_start(cots, sems_c, z)
        for i in {d, (8 - d) % 8}:
            rows = pl.ds(pl.multiple_of(lax.rem(z + 8 - i, 8) * HALF, HALF), HALF)
            part = jnp.dot(hids[i], pw_v[rows, :], preferred_element_type=F32)
            part_b = jnp.dot(hids[i], bw[rows, :], preferred_element_type=F32)
            proj[...] = part if i == 0 else proj[...] + part
            logit[...] = part_b if i == 0 else logit[...] + part_b

    def chunk_pair(step, carry):
        for d in (1, 2, 3):
            pl.when(step == d)(lambda d=d: gather_step(cots, sems_c, z, d))
        r_at, c_at = orders(CR, CR, False, False)
        below = r_at > c_at
        diff = jnp.bitwise_xor(r_at, c_at)
        tr, tc = orders(CT, CR, True, False)
        visible = tc <= 2 * tr + 1
        eye = jnp.where(r_at == c_at, 1.0, 0.0)
        jobs = [(h, 2 * step + cc) for cc in range(2) for h in range(heads)]
        ks, bs, vs, qs = [], [], [], []
        for h, c in jobs:
            a, c1, c2, v1, v2 = head_rows(proj, c, h)
            q = a * unit_scale(a, 1e-6)
            k = jnp.concatenate([c1 * unit_scale(c1, 1e-6), c2 * unit_scale(c2, 1e-6)], axis=0)
            sig, _ = strengths(logit, c, h)
            ks.append(k)
            qs.append(q)
            bs.append(2.0 * sig)
            vs.append(jnp.concatenate([v1, v2], axis=0))
            q_i[h, trows(c), :] = q
            k_i[h, crows(c), :] = k
        kts = [k.T for k in ks]
        kt4 = [rhs(kt) for kt in kts]
        grams = [pmm(lhs(jnp.concatenate([k, q], axis=0)), b4) for k, q, b4 in zip(ks, qs, kt4)]
        for (h, c), g in zip(jobs, grams):
            a_i[h, trows(c), :] = jnp.where(visible, g[CR:], 0.0)
        ns = [jnp.where(below, b * g[:CR], 0.0) for b, g in zip(bs, grams)]
        ts = [eye - jnp.where(diff == 1, n, 0.0) for n in ns]
        level = 1
        while (1 << level) < CR:
            parts = [jnp.where((diff >> level) == 1, n, 0.0) for n in ns]
            inner = [mm(p, t) for p, t in zip(parts, ts)]
            outer = [mm(t, i) for t, i in zip(ts, inner)]
            ts = [t - o for t, o in zip(ts, outer)]
            level += 1
        wus = [mm(t, b * jnp.concatenate([k, v], axis=1)) for t, b, k, v in zip(ts, bs, ks, vs)]
        mos = [pmm(lhs(kt), rhs(wu)) for kt, wu in zip(kts, wus)]
        for (h, c), t, wu, m in zip(jobs, ts, wus, mos):
            t_i[h, crows(c), :] = t
            w_i[h, crows(c), :] = wu[:, :DK]
            uv_i[h, crows(c), :] = wu[:, DK:]
            mc_i[h, crows(c), :] = eye_nat() - m[:, :DK]
            oc[h, crows(c), :] = m[:, DK:]
        return carry

    lax.fori_loop(0, chunks // 2, chunk_pair, 0)

    gather_step(cots, sems_c, z, 4)

    for h in range(heads):
        mo[h, :, :DK] = eye_nat()
        mo[h, :, DK:] = jnp.zeros((DK, DK), F32)

    def prefix(c, carry):
        for h in range(heads):
            cur = mo[h]
            pm_i[h, crows(c), :] = cur[:, :DK]
            po_i[h, crows(c), :] = cur[:, DK:]
            r = mm(mc_i[h, crows(c), :], cur)
            mo[h, :, :DK] = r[:, :DK]
            mo[h, :, DK:] = r[:, DK:] + oc[h, crows(c), :]
        return carry

    lax.fori_loop(0, chunks, prefix, 0)

    c0 = send(mo.at[1 - core], cslot.at[core], sems_f, 0, at(x, y, 1 - core))
    c0.start()
    cslot[core] = mo[core]
    c0.wait()
    first = cslot[0]
    chip = compose(cslot[1], first)
    yslot_f[0] = chip
    sends = [
        send(yslot_f.at[0], yslot_f.at[d], sems_f, d, at(x, lax.rem(y + d, 4), core)) for d in (1, 2, 3)
    ]
    for c in sends:
        c.start()
    ow_copy.wait()
    for i in range(8):
        cols = pl.ds(pl.multiple_of(lax.rem(z + 8 - i, 8) * HALF, HALF), HALF)
        part = lax.dot_general(cots[i], ow_v[:, cols], CONTRACT, preferred_element_type=F32)
        dn[...] = part if i == 0 else dn[...] + part
    for c in sends:
        c.wait()
    got = [yslot_f[lax.rem(y + 4 - i, 4)] for i in range(4)]
    p1 = got[0]
    p2 = compose(got[1], p1)
    p3 = compose(got[2], p2)
    total = compose(got[3], p3)
    xslot_f[0] = total
    sends = [
        send(xslot_f.at[0], xslot_f.at[d], sems_f, 3 + d, at(lax.rem(x + d, 4), y, core))
        for d in (1, 2, 3)
    ]
    for c in sends:
        c.start()
    before = jnp.where(y == 1, p1, jnp.where(y == 2, p2, p3))
    for i in range(2):
        msave_i[i] = cslot[i, :, :DK]
    for i in range(4):
        msave_i[2 + i] = got[i][:, :DK]
    for c in sends:
        c.wait()
    gx = [xslot_f[lax.rem(x + 4 - i, 4)] for i in range(4)]
    for i in range(4):
        msave_i[6 + i] = gx[i][:, :DK]
    s1 = gx[0][:, DK:]
    s2 = mm(gx[1][:, :DK], s1) + gx[1][:, DK:]
    s3 = mm(gx[2][:, :DK], s2) + gx[2][:, DK:]
    group = jnp.where(x == 0, 0.0, jnp.where(x == 1, s1, jnp.where(x == 2, s2, s3)))
    s_chip = jnp.where(y == 0, group, mm(before[:, :DK], group) + before[:, DK:])
    s_next = mm(first[:, :DK], s_chip) + first[:, DK:]
    fin_f[2] = jnp.where(core == 0, s_next, s_chip)
    c1 = send(fin_f.at[2], fin_f.at[core], sems_f, 7, at(x, y, 1 - core))
    c1.start()
    fin_f[core] = jnp.where(core == 0, s_chip, s_next)
    c1.wait()
    start_i[0] = fin_f[0]
    start_i[1] = fin_f[1]


    for h in range(heads):
        esum[h] = jnp.zeros((DK, DK), F32)

    def forward(step, carry):
        jobs = [(h, 2 * step + cc) for cc in range(2) for h in range(heads)]
        starts = [rhs(start_i[h]) for h in range(heads)]
        states = [
            pmm(lhs(pm_i[h, crows(c), :]), starts[h]) + po_i[h, crows(c), :] for h, c in jobs
        ]
        s4 = [rhs(s) for s in states]
        wq = [
            pmm(lhs(jnp.concatenate([w_i[h, crows(c), :], q_i[h, trows(c), :]], axis=0)), b)
            for (h, c), b in zip(jobs, s4)
        ]
        us = [uv_i[h, crows(c), :] - r[:CR] for (h, c), r in zip(jobs, wq)]
        outs = [r[CR:] + mm(a_i[h, trows(c), :], u) for (h, c), r, u in zip(jobs, wq, us)]
        dos = []
        for (h, c), s, u, o in zip(jobs, states, us, outs):
            g = gain[h : h + 1, :]
            r = lax.rsqrt(jnp.mean(o * o, axis=1, keepdims=True) + 1e-5)
            normed[trows(c), h * DK : (h + 1) * DK] = (o * r * g).astype(BF16)
            dy = dn[trows(c), h * DK : (h + 1) * DK] * g
            back = jnp.mean(o * dy, axis=1, keepdims=True)
            do = r * (dy - o * (r * r * back))
            dos.append(do)
            s_s[h, crows(c), :] = s
            u_s[h, crows(c), :] = u
            do_s[h, trows(c), :] = do
        ys = [mmt(a_i[h, trows(c), :], do) for (h, c), do in zip(jobs, dos)]
        es = [
            mmt(q_i[h, trows(c), :], do) - mmt(w_i[h, crows(c), :], yy)
            for (h, c), do, yy in zip(jobs, dos, ys)
        ]
        adds = [mmt(pm_i[h, crows(c), :], e) for (h, c), e in zip(jobs, es)]
        for (h, c), yy, e, add in zip(jobs, ys, es, adds):
            y_s[h, crows(c), :] = yy
            e_s[h, crows(c), :] = e
            esum[h] += add
        return carry

    lax.fori_loop(0, chunks // 2, forward, 0)

    def mixed_term(dest, j):
        cols = pl.ds(pl.multiple_of(dest * HALF, HALF), HALF)
        return jnp.dot(
            normed[j * HALF : (j + 1) * HALF, :], ow_v[:, cols], preferred_element_type=F32
        )

    mixed = Scatter(mixed_term, mixed_o, msent, mcame, sems_m, z)
    c0 = send(esum.at[1 - core], ec.at[core], sems_b, 0, at(x, y, 1 - core))
    c0.start()
    for j in (0, 1):
        for way in (RIGHT, LEFT):
            mixed.step(way, 0, j)
            if j != way:
                mixed.step(way, 1, j)
    ec[core] = esum[core]
    c0.wait()
    e1 = ec[1]
    yslot_b[0] = mmt(msave_i[0], e1) + ec[0]
    sends = [
        send(yslot_b.at[0], yslot_b.at[d], sems_b, d, at(x, lax.rem(y + d, 4), core)) for d in (1, 2, 3)
    ]
    for c in sends:
        c.start()
    my = [msave_i[2 + i] for i in range(4)]
    suf1 = mm(my[3], my[2])
    suf0 = mm(suf1, my[1])
    for way in (RIGHT, LEFT):
        mixed.step(way, 1, way)
    suf = jnp.where(y == 2, my[3], jnp.where(y == 1, suf1, suf0))
    for c in sends:
        c.wait()
    got = [yslot_b[lax.rem(y + 4 - i, 4)] for i in range(4)]
    r3 = got[3]
    r2 = mmt(my[2], r3) + got[2]
    r1 = mmt(my[1], r2) + got[1]
    xslot_b[0] = mmt(my[0], r1) + got[0]
    sends = [
        send(xslot_b.at[0], xslot_b.at[d], sems_b, 3 + d, at(lax.rem(x + d, 4), y, core))
        for d in (1, 2, 3)
    ]
    for c in sends:
        c.start()
    for j in (0, 1):
        for way in (RIGHT, LEFT):
            mixed.step(way, 2, way if j else 1 - way)
    inside = jnp.where(y == 2, r3, jnp.where(y == 1, r2, r1))
    for c in sends:
        c.wait()
    gx = [xslot_b[lax.rem(x + 4 - i, 4)] for i in range(4)]
    x2 = gx[3]
    x1 = mmt(msave_i[8], x2) + gx[2]
    x0 = mmt(msave_i[7], x1) + gx[1]
    group = jnp.where(x == 3, 0.0, jnp.where(x == 2, x2, jnp.where(x == 1, x1, x0)))
    d_chip = jnp.where(y == 3, group, mmt(suf, group) + inside)
    d_prev = mmt(msave_i[1], d_chip) + e1
    fin_b[2] = jnp.where(core == 1, d_prev, d_chip)
    c1 = send(fin_b.at[2], fin_b.at[core], sems_b, 7, at(x, y, 1 - core))
    c1.start()
    fin_b[core] = jnp.where(core == 1, d_chip, d_prev)
    c1.wait()

    def chain(step, carry):
        c = chunks - 1 - step
        for h in range(heads):
            cur = fin_b[h]
            d_s[h, crows(c), :] = cur
            fin_b[h] = mmt(mc_i[h, crows(c), :], cur) + e_s[h, crows(c), :]
        return carry

    lax.fori_loop(0, chunks, chain, 0)

    for j in (0, 1):
        for way in (RIGHT, LEFT):
            mixed.step(way, 3, way if j else 1 - way)

    def grad_term(dest, j):
        rows = slice(j * HALF, (j + 1) * HALF)
        part = pl.ds(pl.multiple_of(dest * HALF, HALF), HALF)
        return lax.dot_general(
            gproj[rows, :], pw_v[part, :], CONTRACT, preferred_element_type=F32
        ) + lax.dot_general(glogit[rows, :], bw[part, :], CONTRACT, preferred_element_type=F32)

    grads = Scatter(grad_term, grad_o, gsent, gcame, sems_g, z)

    def backward(step, carry):
        r_at, c_at = orders(CR, CR, False, False)
        below = r_at > c_at
        tr, tc = orders(CT, CR, True, False)
        visible = tc <= 2 * tr + 1
        jobs = [(h, 2 * step + cc) for cc in range(2) for h in range(heads)]
        ks = [k_i[h, crows(c), :] for h, c in jobs]
        k4 = [rhs(k) for k in ks]
        ds = [d_s[h, crows(c), :] for h, c in jobs]
        us = [u_s[h, crows(c), :] for h, c in jobs]
        dus = [mm(k, d) + y_s[h, crows(c), :] for (h, c), k, d in zip(jobs, ks, ds)]
        zs = [mmt(t_i[h, crows(c), :], du) for (h, c), du in zip(jobs, dus)]
        sigs = [strengths(logit, c, h) for h, c in jobs]
        bzs = [2.0 * sg[0] * z for sg, z in zip(sigs, zs)]
        dos = [do_s[h, trows(c), :] for h, c in jobs]
        both = [lhs(jnp.concatenate([bz, do], axis=0)) for bz, do in zip(bzs, dos)]
        pus = [pmm(b2, rhs(u.T)) for b2, u in zip(both, us)]
        pss = [pmm(b2, rhs(s_s[h, crows(c), :].T)) for (h, c), b2 in zip(jobs, both)]
        pbs = [jnp.where(below, p[:CR], 0.0) for p in pus]
        das = [jnp.where(visible, p[CR:], 0.0) for p in pus]
        mixes = [
            pmm(lhs(jnp.concatenate([pb + pb.T, da], axis=0)), kk)
            for pb, da, kk in zip(pbs, das, k4)
        ]
        dks = [
            mm(u, d.T) - ps[:CR] - mx[:CR] + mmt(da, q_i[h, trows(c), :])
            for (h, c), u, d, ps, mx, da in zip(jobs, us, ds, pss, mixes, das)
        ]
        dqs = [mx[CR:] + ps[CR:] for mx, ps in zip(mixes, pss)]
        for (h, c), k, u, z, bz, sg, dk, dq in zip(jobs, ks, us, zs, bzs, sigs, dks, dqs):
            a, c1, c2, _, _ = head_rows(proj, c, h)
            q = q_i[h, trows(c), :]
            sa = unit_scale(a, 1e-6)
            sc = jnp.concatenate([unit_scale(c1, 1e-6), unit_scale(c2, 1e-6)], axis=0)
            ga = sa * (dq - q * jnp.sum(q * dq, axis=1, keepdims=True))
            gc = sc * (dk - k * jnp.sum(k * dk, axis=1, keepdims=True))
            base = h * 5 * DK
            gproj[trows(c), base : base + DK] = ga.astype(BF16)
            gproj[trows(c), base + DK : base + 2 * DK] = gc[:CT].astype(BF16)
            gproj[trows(c), base + 2 * DK : base + 3 * DK] = gc[CT:].astype(BF16)
            gproj[trows(c), base + 3 * DK : base + 4 * DK] = bz[:CT].astype(BF16)
            gproj[trows(c), base + 4 * DK : base + 5 * DK] = bz[CT:].astype(BF16)
            gl = jnp.sum(z * u, axis=1, keepdims=True) * sg[1]
            glogit[trows(c), 2 * h : 2 * h + 1] = gl[:CT].astype(BF16)
            glogit[trows(c), 2 * h + 1 : 2 * h + 2] = gl[CT:].astype(BF16)
        return carry

    lax.fori_loop(0, chunks // 2, backward, 0)
    mixed.finish()
    for j in (0, 1):
        for way in (RIGHT, LEFT):
            grads.step(way, 0, j)
            if j != way:
                grads.step(way, 1, j)
    for way in (RIGHT, LEFT):
        grads.step(way, 1, way)
    for s in (2, 3):
        for j in (0, 1):
            for way in (RIGHT, LEFT):
                grads.step(way, s, way if j else 1 - way)
    grads.finish()
    gather_end(hids, sems_h, z)
    gather_end(cots, sems_c, z)


def params(collective_id, mib):
    return pltpu.CompilerParams(
        collective_id=collective_id, has_side_effects=True, vmem_limit_bytes=mib << 20
    )


def local(hidden_in, proj_weight, beta_weight, norm_gain, out_weight, cotangent):
    rows = hidden_in.shape[0]
    buf = lambda *shape: pltpu.VMEM(shape, F32)
    low = lambda *shape: pltpu.VMEM(shape, BF16)
    dma = lambda *shape: pltpu.SemaphoreType.DMA(shape)
    part, full = buf(2, rows, DK), buf(2, REFL * rows, DK)
    square, slots = buf(2, DK, DK), buf(4, DK, DK)
    wide, wide_slots = buf(2, DK, 2 * DK), buf(4, DK, 2 * DK)
    out = jax.ShapeDtypeStruct((rows, HALF), BF16)
    anywhere = pl.BlockSpec(memory_space=pl.ANY)
    return pl.pallas_call(
        layer_kernel,
        out_shape=[out, out],
        in_specs=[VM, anywhere, VM, VM, anywhere, VM],
        out_specs=[VM, VM],
        scratch_shapes=[
            low(8, rows, HALF), low(8, rows, HALF), low(*proj_weight.shape), low(*out_weight.shape),
            buf(rows, proj_weight.shape[1]), buf(rows, 4), buf(rows, 2 * DK),
            part, full, full, full, full, part, full, full, full, square, buf(10, DK, DK),
            full, wide, wide, wide_slots, wide_slots, buf(3, DK, DK),
            full, full, part, full, full, full, square, square, slots, slots, buf(3, DK, DK),
            low(rows, 2 * DK), low(rows, 10 * DK), low(rows, 4),
            low(2, 4, rows, HALF), low(2, 4, rows, HALF),
            low(2, 4, rows, HALF), low(2, 4, rows, HALF),
            dma(2, 2, 4, 2), dma(2, 2, 4, 2), dma(2, 8), dma(2, 8),
            dma(2, 2, 4, 2), dma(2, 2, 4, 2), dma(2),
        ],
        compiler_params=params(1, 60),
    )(hidden_in, proj_weight, beta_weight, norm_gain.reshape(2, DK), out_weight, cotangent)


def solution(mesh):
    placed = (
        P("seq", "head"),
        P(None, "head"),
        P(None, "head"),
        P("head"),
        P("head", None),
        P("seq", "head"),
    )
    return jax.shard_map(
        local,
        mesh=mesh,
        in_specs=placed,
        out_specs=(P("seq", "head"), P("seq", "head")),
        check_vma=False,
    )
```

time: 250 us -> 143 us (0.57)
  waiting for transfers between devices: 127 us -> 0 us
  Pallas kernels: 79.6 us -> 136 us
  matrix products: 21.5 us -> 0 us
  between operations: 13.9 us -> 0.64 us
    reduce_scatter x2 -> x0, waiting for transfers between devices: 75.7 us -> none  [the longest x1 44 us: local(): lax.psum_scatter(input_term.astype(BF16), 'head', scatter_dimension=1, ti...]
    pallas_call x2 -> x1, Pallas kernels: 79.6 us -> 136 us  [local(): pl.pallas_call(layer_kernel, out_shape=[out, out], in_specs=[VM, anywhere...]
    all_gather x2 -> x0, waiting for transfers between devices: 50.1 us -> none  [the longest x1 50.1 us: local(): hidden_part = lax.all_gather(hidden_in, 'head', axis=1, tiled=True)]
    dot_general x6 -> x0, matrix products: 21.5 us -> none  [the longest x1 7.63 us: local(): projected = jnp.dot(hidden_part, proj_weight, preferred_element_type=F32)]
    unnamed x26 -> x3, local copies, waits for them, and re-layouts: 6.02 us -> 5.1 us
  transfers between devices with their start and end apart: 4 -> 0, of which waited for: 3 -> 0; matrix products, arithmetic and copies ran while one was open for 3% -> 0% of each run, Pallas kernels for 17% -> 0%
where the time goes in v2:
time: 143 us; the launch traced here: 142 us
  Pallas kernels  136 us (95%)
  local copies, waits for them, and re-layouts  5.1 us (4%)
    pallas_call x1, Pallas kernels, local(): pl.pallas_call(layer_kernel, out_shape=[out, out], in_specs=[VM, anywhere...  136 us
    unnamed x3, local copies, waits for them, and re-layouts  5.1 us

profile of v2, /device:TPU:64, one launch (start us, length us, event | category | flops | bytes accessed | tf_op | source)
XLA Modules:
  0.0 141.9 jit_solution(11049747374276612924)
XLA Ops:
  0.6 1.8 %copy.8.bw = bf16[2048,4]{1,0:T(8,128)(2,1)} copy(bf16[2048,4]{0,1:T(4,128)(2,1)} %param.8) | data formatting | bytes 32768 | tf_op args[2]
  2.4 136.1 %shard_map.77 = (bf16[512,256]{1,0:T(8,128)(2,1)}, bf16[512,256]{1,0:T(8,128)(2,1)}) custom-call(bf16[512,256]{1,0:T(8,128)(2,1)} %hid.1, bf16[2048,1280]{1,0:T(8,128)(2,1)} %pw.1, bf16[2048,4]{1,0:T(8,128)(2,1)} %copy.8.bw, f32[2,128]{1,0:T(2,128)} %bitcast.1, bf16[256,2048]{1,0:T(8,128)(2,1)} %ow.1, bf16[512,256]{1,0:T(8,128)(2,1)} %cot.1), custom_call_target="tpu_custom_call" | custom-call | tf_op jit(solution)/shard_map/pallas_call | solution.py:594
  138.5 1.7 %copy.11 = bf16[512,256]{1,0:T(8,128)(2,1)} copy(bf16[512,256]{1,0:T(8,128)(2,1)} %get-tuple-element.4) | data formatting | bytes 524288
  140.2 1.7 %copy.12 = bf16[512,256]{1,0:T(8,128)(2,1)} copy(bf16[512,256]{1,0:T(8,128)(2,1)} %get-tuple-element.5) | data formatting | bytes 524288

commit v3 on v2

--- a/solution.py
+++ b/solution.py
@@ -44,6 +44,13 @@
 
 def mmt(a, b):
     return pmm(lhs(a.T), rhs(b))
+
+
+def mmb(a, b):
+    hi, lo = split(b)
+    n = b.shape[1]
+    r = jnp.dot(a, jnp.concatenate([hi, lo], axis=1), preferred_element_type=F32)
+    return r[:, :n] + r[:, n:]
 
 
 def orders(rows, cols, row_tokens, col_tokens):
@@ -157,8 +164,9 @@
 
 
 class Scatter:
-    def __init__(self, own, out, sent, came, sems, z):
-        self.own, self.out, self.sent, self.came, self.sems, self.z = own, out, sent, came, sems, z
+    def __init__(self, own, out, col, sent, came, sems, z):
+        self.own, self.out, self.col, self.z = own, out, col, z
+        self.sent, self.came, self.sems = sent, came, sems
 
     def unit(self, way, s, j):
         rows = pl.ds(j * HALF, HALF)
@@ -186,14 +194,15 @@
         self.sent[way, s, rows] = term.astype(BF16)
         self.unit(way, s, j).start()
 
-    def finish(self):
-        for j in (0, 1):
-            rows = slice(j * HALF, (j + 1) * HALF)
-            term = self.own(self.z, j)
-            for way in (RIGHT, LEFT):
-                self.unit(way, 3, j).wait_recv()
-                term = term + self.came[way, 3, rows].astype(F32)
-            self.out[rows, :] = term.astype(BF16)
+    def finish(self, j):
+        rows = slice(j * HALF, (j + 1) * HALF)
+        term = self.own(self.z, j)
+        for way in (RIGHT, LEFT):
+            self.unit(way, 3, j).wait_recv()
+            term = term + self.came[way, 3, rows].astype(F32)
+        self.out[rows, self.col : self.col + HALF] = term.astype(BF16)
+
+    def end(self):
         for way in (RIGHT, LEFT):
             for s in range(4):
                 for j in (0, 1):
@@ -212,9 +221,9 @@
     )
 
 
-def compose(later, earlier):
-    r = mm(later[:, :DK], earlier)
-    return jnp.concatenate([r[:, :DK], r[:, DK:] + later[:, DK:]], axis=1)
+def compose(later, earlier, times=mm):
+    r = times(later[:, :DK], earlier)
+    return jnp.concatenate([r[:, :DK], r[:, DK:] + later[:, DK:].astype(F32)], axis=1)
 
 
 def eye_nat():
@@ -228,9 +237,9 @@
 
 def layer_kernel(
     hid, pw, bw, gain, ow, cot,
-    mixed_o, grad_o,
+    out,
     hids, cots, pw_v, ow_v, proj, logit, dn,
-    q_i, k_i, w_i, uv_i, t_i, a_i, pm_i, po_i, mc_i, start_i, msave_i,
+    q_i, k_i, w_i, uv_i, t_i, a_i, pm_i, po_i, mc_i, msave, qp_s, q2_s, o2_s,
     oc, mo, cslot, yslot_f, xslot_f, fin_f,
     s_s, u_s, do_s, y_s, e_s, d_s, esum, ec, yslot_b, xslot_b, fin_b,
     normed, gproj, glogit, msent, mcame, gsent, gcame,
@@ -258,7 +267,7 @@
         for i in {d, (8 - d) % 8}:
             rows = pl.ds(pl.multiple_of(lax.rem(z + 8 - i, 8) * HALF, HALF), HALF)
             part = jnp.dot(hids[i], pw_v[rows, :], preferred_element_type=F32)
-            part_b = jnp.dot(hids[i], bw[rows, :], preferred_element_type=F32)
+            part_b = lax.dot_general(hids[i], bw[:, rows], CONTRACT, preferred_element_type=F32)
             proj[...] = part if i == 0 else proj[...] + part
             logit[...] = part_b if i == 0 else logit[...] + part_b
 
@@ -310,8 +319,6 @@
 
     lax.fori_loop(0, chunks // 2, chunk_pair, 0)
 
-    gather_step(cots, sems_c, z, 4)
-
     for h in range(heads):
         mo[h, :, :DK] = eye_nat()
         mo[h, :, DK:] = jnp.zeros((DK, DK), F32)
@@ -333,26 +340,37 @@
     cslot[core] = mo[core]
     c0.wait()
     first = cslot[0]
-    chip = compose(cslot[1], first)
-    yslot_f[0] = chip
+    yslot_f[0] = compose(cslot[1], first).astype(BF16)
     sends = [
-        send(yslot_f.at[0], yslot_f.at[d], sems_f, d, at(x, lax.rem(y + d, 4), core)) for d in (1, 2, 3)
+        send(yslot_f.at[0], yslot_f.at[d], sems_f, d, at(x, lax.rem(y + d, 4), core))
+        for d in (1, 2, 3)
     ]
     for c in sends:
         c.start()
-    ow_copy.wait()
-    for i in range(8):
-        cols = pl.ds(pl.multiple_of(lax.rem(z + 8 - i, 8) * HALF, HALF), HALF)
-        part = lax.dot_general(cots[i], ow_v[:, cols], CONTRACT, preferred_element_type=F32)
-        dn[...] = part if i == 0 else dn[...] + part
+
+    def read_maps(step, carry):
+        jobs = [(h, 2 * step + cc) for cc in range(2) for h in range(heads)]
+        sees = [lhs(a_i[h, trows(c), :]) for h, c in jobs]
+        aws = [pmm(a2, rhs(w_i[h, crows(c), :])) for (h, c), a2 in zip(jobs, sees)]
+        aus = [pmm(a2, rhs(uv_i[h, crows(c), :])) for (h, c), a2 in zip(jobs, sees)]
+        qps = [q_i[h, trows(c), :] - aw for (h, c), aw in zip(jobs, aws)]
+        qp2 = [lhs(qp) for qp in qps]
+        q2s = [pmm(a2, rhs(pm_i[h, crows(c), :])) for (h, c), a2 in zip(jobs, qp2)]
+        o2s = [pmm(a2, rhs(po_i[h, crows(c), :])) for (h, c), a2 in zip(jobs, qp2)]
+        for (h, c), qp, q2, o2, au in zip(jobs, qps, q2s, o2s, aus):
+            qp_s[h, trows(c), :] = qp
+            q2_s[h, trows(c), :] = q2
+            o2_s[h, trows(c), :] = o2 + au
+        return carry
+
+    lax.fori_loop(0, chunks // 2, read_maps, 0)
     for c in sends:
         c.wait()
     got = [yslot_f[lax.rem(y + 4 - i, 4)] for i in range(4)]
-    p1 = got[0]
-    p2 = compose(got[1], p1)
-    p3 = compose(got[2], p2)
-    total = compose(got[3], p3)
-    xslot_f[0] = total
+    p1 = got[0].astype(F32)
+    p2 = compose(got[1], p1, mmb)
+    p3 = compose(got[2], p2, mmb)
+    xslot_f[0] = compose(got[3], p3, mmb).astype(BF16)
     sends = [
         send(xslot_f.at[0], xslot_f.at[d], sems_f, 3 + d, at(lax.rem(x + d, 4), y, core))
         for d in (1, 2, 3)
@@ -360,18 +378,24 @@
     for c in sends:
         c.start()
     before = jnp.where(y == 1, p1, jnp.where(y == 2, p2, p3))
-    for i in range(2):
-        msave_i[i] = cslot[i, :, :DK]
+    m_y = [g[:, :DK].T for g in got]
+    suf1 = mmb(m_y[2], m_y[3].astype(F32))
+    suf0 = mmb(m_y[1], suf1)
+    suf = jnp.where(y == 2, m_y[3].astype(F32), jnp.where(y == 1, suf1, suf0))
     for i in range(4):
-        msave_i[2 + i] = got[i][:, :DK]
+        msave[i] = m_y[i]
+    gather_step(cots, sems_c, z, 4)
+    ow_copy.wait()
+    for i in range(8):
+        cols = pl.ds(pl.multiple_of(lax.rem(z + 8 - i, 8) * HALF, HALF), HALF)
+        term = lax.dot_general(cots[i], ow_v[:, cols], CONTRACT, preferred_element_type=F32)
+        dn[...] = term if i == 0 else dn[...] + term
     for c in sends:
         c.wait()
     gx = [xslot_f[lax.rem(x + 4 - i, 4)] for i in range(4)]
-    for i in range(4):
-        msave_i[6 + i] = gx[i][:, :DK]
-    s1 = gx[0][:, DK:]
-    s2 = mm(gx[1][:, :DK], s1) + gx[1][:, DK:]
-    s3 = mm(gx[2][:, :DK], s2) + gx[2][:, DK:]
+    s1 = gx[0][:, DK:].astype(F32)
+    s2 = mmb(gx[1][:, :DK], s1) + gx[1][:, DK:].astype(F32)
+    s3 = mmb(gx[2][:, :DK], s2) + gx[2][:, DK:].astype(F32)
     group = jnp.where(x == 0, 0.0, jnp.where(x == 1, s1, jnp.where(x == 2, s2, s3)))
     s_chip = jnp.where(y == 0, group, mm(before[:, :DK], group) + before[:, DK:])
     s_next = mm(first[:, :DK], s_chip) + first[:, DK:]
@@ -380,51 +404,14 @@
     c1.start()
     fin_f[core] = jnp.where(core == 0, s_chip, s_next)
     c1.wait()
-    start_i[0] = fin_f[0]
-    start_i[1] = fin_f[1]
-
-
+
+    outs, scales = [], []
     for h in range(heads):
-        esum[h] = jnp.zeros((DK, DK), F32)
-
-    def forward(step, carry):
-        jobs = [(h, 2 * step + cc) for cc in range(2) for h in range(heads)]
-        starts = [rhs(start_i[h]) for h in range(heads)]
-        states = [
-            pmm(lhs(pm_i[h, crows(c), :]), starts[h]) + po_i[h, crows(c), :] for h, c in jobs
-        ]
-        s4 = [rhs(s) for s in states]
-        wq = [
-            pmm(lhs(jnp.concatenate([w_i[h, crows(c), :], q_i[h, trows(c), :]], axis=0)), b)
-            for (h, c), b in zip(jobs, s4)
-        ]
-        us = [uv_i[h, crows(c), :] - r[:CR] for (h, c), r in zip(jobs, wq)]
-        outs = [r[CR:] + mm(a_i[h, trows(c), :], u) for (h, c), r, u in zip(jobs, wq, us)]
-        dos = []
-        for (h, c), s, u, o in zip(jobs, states, us, outs):
-            g = gain[h : h + 1, :]
-            r = lax.rsqrt(jnp.mean(o * o, axis=1, keepdims=True) + 1e-5)
-            normed[trows(c), h * DK : (h + 1) * DK] = (o * r * g).astype(BF16)
-            dy = dn[trows(c), h * DK : (h + 1) * DK] * g
-            back = jnp.mean(o * dy, axis=1, keepdims=True)
-            do = r * (dy - o * (r * r * back))
-            dos.append(do)
-            s_s[h, crows(c), :] = s
-            u_s[h, crows(c), :] = u
-            do_s[h, trows(c), :] = do
-        ys = [mmt(a_i[h, trows(c), :], do) for (h, c), do in zip(jobs, dos)]
-        es = [
-            mmt(q_i[h, trows(c), :], do) - mmt(w_i[h, crows(c), :], yy)
-            for (h, c), do, yy in zip(jobs, dos, ys)
-        ]
-        adds = [mmt(pm_i[h, crows(c), :], e) for (h, c), e in zip(jobs, es)]
-        for (h, c), yy, e, add in zip(jobs, ys, es, adds):
-            y_s[h, crows(c), :] = yy
-            e_s[h, crows(c), :] = e
-            esum[h] += add
-        return carry
-
-    lax.fori_loop(0, chunks // 2, forward, 0)
+        o = mm(q2_s[h], fin_f[h]) + o2_s[h]
+        r = lax.rsqrt(jnp.mean(o * o, axis=1, keepdims=True) + 1e-5)
+        normed[:, h * DK : (h + 1) * DK] = (o * r * gain[h : h + 1, :]).astype(BF16)
+        outs.append(o)
+        scales.append(r)
 
     def mixed_term(dest, j):
         cols = pl.ds(pl.multiple_of(dest * HALF, HALF), HALF)
@@ -432,59 +419,95 @@
             normed[j * HALF : (j + 1) * HALF, :], ow_v[:, cols], preferred_element_type=F32
         )
 
-    mixed = Scatter(mixed_term, mixed_o, msent, mcame, sems_m, z)
+    mixed = Scatter(mixed_term, out, 0, msent, mcame, sems_m, z)
+    mixed.step(RIGHT, 0, 0)
+    mixed.step(LEFT, 0, 1)
+    mixed.step(RIGHT, 1, 1)
+    mixed.step(LEFT, 1, 0)
+    for h in range(heads):
+        o, r = outs[h], scales[h]
+        dy = dn[:, h * DK : (h + 1) * DK] * gain[h : h + 1, :]
+        back = jnp.mean(o * dy, axis=1, keepdims=True)
+        do = r * (dy - o * (r * r * back))
+        do_s[h] = do
+        esum[h] = mmt(q2_s[h], do)
+
     c0 = send(esum.at[1 - core], ec.at[core], sems_b, 0, at(x, y, 1 - core))
     c0.start()
-    for j in (0, 1):
-        for way in (RIGHT, LEFT):
-            mixed.step(way, 0, j)
-            if j != way:
-                mixed.step(way, 1, j)
     ec[core] = esum[core]
+    m_c = [cslot[i, :, :DK].T for i in range(2)]
     c0.wait()
     e1 = ec[1]
-    yslot_b[0] = mmt(msave_i[0], e1) + ec[0]
+    yslot_b[0] = (mm(m_c[0], e1) + ec[0]).astype(BF16)
     sends = [
-        send(yslot_b.at[0], yslot_b.at[d], sems_b, d, at(x, lax.rem(y + d, 4), core)) for d in (1, 2, 3)
+        send(yslot_b.at[0], yslot_b.at[d], sems_b, d, at(x, lax.rem(y + d, 4), core))
+        for d in (1, 2, 3)
     ]
     for c in sends:
         c.start()
-    my = [msave_i[2 + i] for i in range(4)]
-    suf1 = mm(my[3], my[2])
-    suf0 = mm(suf1, my[1])
-    for way in (RIGHT, LEFT):
-        mixed.step(way, 1, way)
-    suf = jnp.where(y == 2, my[3], jnp.where(y == 1, suf1, suf0))
+
+    def inner_parts(step, carry):
+        @pl.when(step == 1)
+        def _():
+            mixed.step(RIGHT, 1, 0)
+            mixed.step(LEFT, 1, 1)
+
+        @pl.when(step == 3)
+        def _():
+            mixed.step(RIGHT, 2, 1)
+            mixed.step(LEFT, 2, 0)
+
+        jobs = [(h, 2 * step + cc) for cc in range(2) for h in range(heads)]
+        starts = [rhs(fin_f[h]) for h in range(heads)]
+        states = [
+            pmm(lhs(pm_i[h, crows(c), :]), starts[h]) + po_i[h, crows(c), :] for h, c in jobs
+        ]
+        us = [uv_i[h, crows(c), :] - mm(w_i[h, crows(c), :], s) for (h, c), s in zip(jobs, states)]
+        dos = [do_s[h, trows(c), :] for h, c in jobs]
+        sides = [
+            mmt(jnp.concatenate([a_i[h, trows(c), :], qp_s[h, trows(c), :]], axis=1), do)
+            for (h, c), do in zip(jobs, dos)
+        ]
+        for (h, c), s, u, side in zip(jobs, states, us, sides):
+            s_s[h, crows(c), :] = s
+            u_s[h, crows(c), :] = u
+            y_s[h, crows(c), :] = side[:CR]
+            e_s[h, crows(c), :] = side[CR:]
+        return carry
+
+    lax.fori_loop(0, chunks // 2, inner_parts, 0)
     for c in sends:
         c.wait()
     got = [yslot_b[lax.rem(y + 4 - i, 4)] for i in range(4)]
-    r3 = got[3]
-    r2 = mmt(my[2], r3) + got[2]
-    r1 = mmt(my[1], r2) + got[1]
-    xslot_b[0] = mmt(my[0], r1) + got[0]
+    r3 = got[3].astype(F32)
+    r2 = mmb(msave[2], r3) + got[2].astype(F32)
+    r1 = mmb(msave[1], r2) + got[1].astype(F32)
+    xslot_b[0] = (mmb(msave[0], r1) + got[0].astype(F32)).astype(BF16)
     sends = [
         send(xslot_b.at[0], xslot_b.at[d], sems_b, 3 + d, at(lax.rem(x + d, 4), y, core))
         for d in (1, 2, 3)
     ]
     for c in sends:
         c.start()
-    for j in (0, 1):
-        for way in (RIGHT, LEFT):
-            mixed.step(way, 2, way if j else 1 - way)
     inside = jnp.where(y == 2, r3, jnp.where(y == 1, r2, r1))
+    m_x = [xslot_f[lax.rem(x + 4 - i, 4), :, :DK].T for i in (1, 2)]
+    mixed.step(RIGHT, 2, 0)
+    mixed.step(LEFT, 2, 1)
     for c in sends:
         c.wait()
-    gx = [xslot_b[lax.rem(x + 4 - i, 4)] for i in range(4)]
+    gx = [xslot_b[lax.rem(x + 4 - i, 4)].astype(F32) for i in range(4)]
     x2 = gx[3]
-    x1 = mmt(msave_i[8], x2) + gx[2]
-    x0 = mmt(msave_i[7], x1) + gx[1]
+    x1 = mmb(m_x[1], x2) + gx[2]
+    x0 = mmb(m_x[0], x1) + gx[1]
     group = jnp.where(x == 3, 0.0, jnp.where(x == 2, x2, jnp.where(x == 1, x1, x0)))
-    d_chip = jnp.where(y == 3, group, mmt(suf, group) + inside)
-    d_prev = mmt(msave_i[1], d_chip) + e1
+    d_chip = jnp.where(y == 3, group, mm(suf, group) + inside)
+    d_prev = mm(m_c[1], d_chip) + e1
     fin_b[2] = jnp.where(core == 1, d_prev, d_chip)
     c1 = send(fin_b.at[2], fin_b.at[core], sems_b, 7, at(x, y, 1 - core))
     c1.start()
     fin_b[core] = jnp.where(core == 1, d_chip, d_prev)
+    mixed.step(RIGHT, 3, 1)
+    mixed.step(LEFT, 3, 0)
     c1.wait()
 
     def chain(step, carry):
@@ -497,20 +520,31 @@
 
     lax.fori_loop(0, chunks, chain, 0)
 
-    for j in (0, 1):
-        for way in (RIGHT, LEFT):
-            mixed.step(way, 3, way if j else 1 - way)
-
     def grad_term(dest, j):
         rows = slice(j * HALF, (j + 1) * HALF)
         part = pl.ds(pl.multiple_of(dest * HALF, HALF), HALF)
         return lax.dot_general(
             gproj[rows, :], pw_v[part, :], CONTRACT, preferred_element_type=F32
-        ) + lax.dot_general(glogit[rows, :], bw[part, :], CONTRACT, preferred_element_type=F32)
-
-    grads = Scatter(grad_term, grad_o, gsent, gcame, sems_g, z)
+        ) + jnp.dot(glogit[rows, :], bw[:, part], preferred_element_type=F32)
+
+    grads = Scatter(grad_term, out, HALF, gsent, gcame, sems_g, z)
 
     def backward(step, carry):
+        @pl.when(step == 1)
+        def _():
+            mixed.step(RIGHT, 3, 0)
+            mixed.step(LEFT, 3, 1)
+
+        @pl.when(step == 2)
+        def _():
+            grads.step(RIGHT, 0, 0)
+            grads.step(LEFT, 1, 0)
+
+        @pl.when(step == 3)
+        def _():
+            grads.step(RIGHT, 1, 0)
+            grads.step(LEFT, 2, 0)
+
         r_at, c_at = orders(CR, CR, False, False)
         below = r_at > c_at
         tr, tc = orders(CT, CR, True, False)
@@ -558,19 +592,22 @@
         return carry
 
     lax.fori_loop(0, chunks // 2, backward, 0)
-    mixed.finish()
-    for j in (0, 1):
-        for way in (RIGHT, LEFT):
-            grads.step(way, 0, j)
-            if j != way:
-                grads.step(way, 1, j)
-    for way in (RIGHT, LEFT):
-        grads.step(way, 1, way)
-    for s in (2, 3):
-        for j in (0, 1):
-            for way in (RIGHT, LEFT):
-                grads.step(way, s, way if j else 1 - way)
-    grads.finish()
+    mixed.finish(0)
+    mixed.finish(1)
+    grads.step(RIGHT, 1, 1)
+    grads.step(LEFT, 0, 1)
+    grads.step(RIGHT, 2, 0)
+    grads.step(LEFT, 3, 0)
+    grads.step(RIGHT, 2, 1)
+    grads.step(LEFT, 1, 1)
+    grads.step(RIGHT, 3, 0)
+    grads.step(LEFT, 2, 1)
+    grads.step(RIGHT, 3, 1)
+    grads.step(LEFT, 3, 1)
+    grads.finish(0)
+    grads.finish(1)
+    mixed.end()
+    grads.end()
     gather_end(hids, sems_h, z)
     gather_end(cots, sems_c, z)
 
@@ -587,21 +624,19 @@
     low = lambda *shape: pltpu.VMEM(shape, BF16)
     dma = lambda *shape: pltpu.SemaphoreType.DMA(shape)
     part, full = buf(2, rows, DK), buf(2, REFL * rows, DK)
-    square, slots = buf(2, DK, DK), buf(4, DK, DK)
-    wide, wide_slots = buf(2, DK, 2 * DK), buf(4, DK, 2 * DK)
-    out = jax.ShapeDtypeStruct((rows, HALF), BF16)
+    square, wide = buf(2, DK, DK), buf(2, DK, 2 * DK)
     anywhere = pl.BlockSpec(memory_space=pl.ANY)
-    return pl.pallas_call(
+    both = pl.pallas_call(
         layer_kernel,
-        out_shape=[out, out],
+        out_shape=jax.ShapeDtypeStruct((rows, 2 * HALF), BF16),
         in_specs=[VM, anywhere, VM, VM, anywhere, VM],
-        out_specs=[VM, VM],
+        out_specs=VM,
         scratch_shapes=[
             low(8, rows, HALF), low(8, rows, HALF), low(*proj_weight.shape), low(*out_weight.shape),
             buf(rows, proj_weight.shape[1]), buf(rows, 4), buf(rows, 2 * DK),
-            part, full, full, full, full, part, full, full, full, square, buf(10, DK, DK),
-            full, wide, wide, wide_slots, wide_slots, buf(3, DK, DK),
-            full, full, part, full, full, full, square, square, slots, slots, buf(3, DK, DK),
+            part, full, full, full, full, part, full, full, full, low(4, DK, DK), part, part, part,
+            full, wide, wide, low(4, DK, 2 * DK), low(4, DK, 2 * DK), buf(3, DK, DK),
+            full, full, part, full, full, full, square, square, low(4, DK, DK), low(4, DK, DK), buf(3, DK, DK),
             low(rows, 2 * DK), low(rows, 10 * DK), low(rows, 4),
             low(2, 4, rows, HALF), low(2, 4, rows, HALF),
             low(2, 4, rows, HALF), low(2, 4, rows, HALF),
@@ -609,7 +644,8 @@
             dma(2, 2, 4, 2), dma(2, 2, 4, 2), dma(2),
         ],
         compiler_params=params(1, 60),
-    )(hidden_in, proj_weight, beta_weight, norm_gain.reshape(2, DK), out_weight, cotangent)
+    )(hidden_in, proj_weight, beta_weight.T, norm_gain.reshape(2, DK), out_weight, cotangent)
+    return both[:, :HALF], both[:, HALF:]
 
 
 def solution(mesh):

time: 143 us -> 128 us (0.90); the launches traced: 142 us -> 128 us
  Pallas kernels: 136 us -> 126 us
  local copies, waits for them, and re-layouts: 5.1 us -> 1.85 us
    pallas_call x1, Pallas kernels: 136 us -> 126 us  [local(): pl.pallas_call(layer_kernel, out_shape=jax.ShapeDtypeStruct((rows, 2 * HA...]
    unnamed x3 -> x0, local copies, waits for them, and re-layouts: 5.1 us -> none
    slice x0 -> x1, local copies, waits for them, and re-layouts: none -> 1.85 us  [local(): return (both[:, :HALF], both[:, HALF:])]
where the time goes in v3:
time: 128 us
  Pallas kernels  126 us (98%)
  local copies, waits for them, and re-layouts  1.85 us (1%)
    pallas_call x1, Pallas kernels, local(): pl.pallas_call(layer_kernel, out_shape=jax.ShapeDtypeStruct((rows, 2 * HA...  126 us

profile of v3, /device:TPU:64, one launch (start us, length us, event | category | flops | bytes accessed | tf_op | source)
XLA Modules:
  0.0 128.3 jit_solution(14485417331303662274)
XLA Ops:
  0.6 125.8 %shard_map.77 = bf16[512,512]{1,0:T(8,128)(2,1)} custom-call(bf16[512,256]{1,0:T(8,128)(2,1)} %hid.1, bf16[2048,1280]{1,0:T(8,128)(2,1)} %pw.1, bf16[4,2048]{1,0:T(4,128)(2,1)} %bitcast.2, f32[2,128]{1,0:T(2,128)} %bitcast.3, bf16[256,2048]{1,0:T(8,128)(2,1)} %ow.1, bf16[512,256]{1,0:T(8,128)(2,1)} %cot.1), custom_call_target="tpu_custom_call" | custom-call | tf_op jit(solution)/shard_map/pallas_call | solution.py:629
  126.5 1.9 %fusion = (bf16[512,256]{1,0:T(8,128)(2,1)}, bf16[512,256]{1,0:T(8,128)(2,1)}) fusion(bf16[512,512]{1,0:T(8,128)(2,1)} %shard_map.77), kind=kLoop, calls=%fused_computation | loop fusion | bytes 1048576 | tf_op jit(solution)/shard_map/slice | solution.py:648

commit v4 on v3

--- a/solution.py
+++ b/solution.py
@@ -9,6 +9,7 @@
 REFL = 2
 CT = 64
 CR = CT * REFL
+BATCH = 4
 MESH = pl.DeviceIdType.MESH
 F32 = jnp.float32
 BF16 = jnp.bfloat16
@@ -146,8 +147,8 @@
             gather_unit(buf, sems, z, way, 1, j).start()
 
 
-def gather_step(buf, sems, z, d):
-    for j in (0, 1):
+def gather_step(buf, sems, z, d, halves=(0, 1)):
+    for j in halves:
         for way in (RIGHT, LEFT):
             if gather_has(way, d, j):
                 gather_unit(buf, sems, z, way, d, j).wait_recv()
@@ -262,7 +263,7 @@
     for d in range(5):
         if d > 0:
             gather_step(hids, sems_h, z, d)
-        if d == 3:
+        if d == 4:
             gather_start(cots, sems_c, z)
         for i in {d, (8 - d) % 8}:
             rows = pl.ds(pl.multiple_of(lax.rem(z + 8 - i, 8) * HALF, HALF), HALF)
@@ -271,16 +272,18 @@
             proj[...] = part if i == 0 else proj[...] + part
             logit[...] = part_b if i == 0 else logit[...] + part_b
 
-    def chunk_pair(step, carry):
-        for d in (1, 2, 3):
-            pl.when(step == d)(lambda d=d: gather_step(cots, sems_c, z, d))
+    def chunk_batch(step, carry):
+        @pl.when(step == 1)
+        def _():
+            gather_step(cots, sems_c, z, 1, (0,))
+
         r_at, c_at = orders(CR, CR, False, False)
         below = r_at > c_at
         diff = jnp.bitwise_xor(r_at, c_at)
         tr, tc = orders(CT, CR, True, False)
         visible = tc <= 2 * tr + 1
         eye = jnp.where(r_at == c_at, 1.0, 0.0)
-        jobs = [(h, 2 * step + cc) for cc in range(2) for h in range(heads)]
+        jobs = [(h, BATCH * step + cc) for cc in range(BATCH) for h in range(heads)]
         ks, bs, vs, qs = [], [], [], []
         for h, c in jobs:
             a, c1, c2, v1, v2 = head_rows(proj, c, h)
@@ -317,7 +320,9 @@
             oc[h, crows(c), :] = m[:, DK:]
         return carry
 
-    lax.fori_loop(0, chunks // 2, chunk_pair, 0)
+    lax.fori_loop(0, chunks // BATCH, chunk_batch, 0)
+
+    gather_step(cots, sems_c, z, 1, (1,))
 
     for h in range(heads):
         mo[h, :, :DK] = eye_nat()
@@ -338,6 +343,7 @@
     c0 = send(mo.at[1 - core], cslot.at[core], sems_f, 0, at(x, y, 1 - core))
     c0.start()
     cslot[core] = mo[core]
+    gather_step(cots, sems_c, z, 2, (0,))
     c0.wait()
     first = cslot[0]
     yslot_f[0] = compose(cslot[1], first).astype(BF16)
@@ -348,8 +354,14 @@
     for c in sends:
         c.start()
 
+    gather_step(cots, sems_c, z, 2, (1,))
+
     def read_maps(step, carry):
-        jobs = [(h, 2 * step + cc) for cc in range(2) for h in range(heads)]
+        @pl.when(step == 1)
+        def _():
+            gather_step(cots, sems_c, z, 3, (0,))
+
+        jobs = [(h, BATCH * step + cc) for cc in range(BATCH) for h in range(heads)]
         sees = [lhs(a_i[h, trows(c), :]) for h, c in jobs]
         aws = [pmm(a2, rhs(w_i[h, crows(c), :])) for (h, c), a2 in zip(jobs, sees)]
         aus = [pmm(a2, rhs(uv_i[h, crows(c), :])) for (h, c), a2 in zip(jobs, sees)]
@@ -363,9 +375,10 @@
             o2_s[h, trows(c), :] = o2 + au
         return carry
 
-    lax.fori_loop(0, chunks // 2, read_maps, 0)
+    lax.fori_loop(0, chunks // BATCH, read_maps, 0)
     for c in sends:
         c.wait()
+    gather_step(cots, sems_c, z, 3, (1,))
     got = [yslot_f[lax.rem(y + 4 - i, 4)] for i in range(4)]
     p1 = got[0].astype(F32)
     p2 = compose(got[1], p1, mmb)
@@ -452,12 +465,7 @@
             mixed.step(RIGHT, 1, 0)
             mixed.step(LEFT, 1, 1)
 
-        @pl.when(step == 3)
-        def _():
-            mixed.step(RIGHT, 2, 1)
-            mixed.step(LEFT, 2, 0)
-
-        jobs = [(h, 2 * step + cc) for cc in range(2) for h in range(heads)]
+        jobs = [(h, BATCH * step + cc) for cc in range(BATCH) for h in range(heads)]
         starts = [rhs(fin_f[h]) for h in range(heads)]
         states = [
             pmm(lhs(pm_i[h, crows(c), :]), starts[h]) + po_i[h, crows(c), :] for h, c in jobs
@@ -475,7 +483,9 @@
             e_s[h, crows(c), :] = side[CR:]
         return carry
 
-    lax.fori_loop(0, chunks // 2, inner_parts, 0)
+    lax.fori_loop(0, chunks // BATCH, inner_parts, 0)
+    mixed.step(RIGHT, 2, 1)
+    mixed.step(LEFT, 2, 0)
     for c in sends:
         c.wait()
     got = [yslot_b[lax.rem(y + 4 - i, 4)] for i in range(4)]
@@ -534,22 +544,14 @@
         def _():
             mixed.step(RIGHT, 3, 0)
             mixed.step(LEFT, 3, 1)
-
-        @pl.when(step == 2)
-        def _():
             grads.step(RIGHT, 0, 0)
             grads.step(LEFT, 1, 0)
-
-        @pl.when(step == 3)
-        def _():
-            grads.step(RIGHT, 1, 0)
-            grads.step(LEFT, 2, 0)
 
         r_at, c_at = orders(CR, CR, False, False)
         below = r_at > c_at
         tr, tc = orders(CT, CR, True, False)
         visible = tc <= 2 * tr + 1
-        jobs = [(h, 2 * step + cc) for cc in range(2) for h in range(heads)]
+        jobs = [(h, BATCH * step + cc) for cc in range(BATCH) for h in range(heads)]
         ks = [k_i[h, crows(c), :] for h, c in jobs]
         k4 = [rhs(k) for k in ks]
         ds = [d_s[h, crows(c), :] for h, c in jobs]
@@ -591,11 +593,13 @@
             glogit[trows(c), 2 * h + 1 : 2 * h + 2] = gl[CT:].astype(BF16)
         return carry
 
-    lax.fori_loop(0, chunks // 2, backward, 0)
+    lax.fori_loop(0, chunks // BATCH, backward, 0)
+    grads.step(RIGHT, 1, 1)
+    grads.step(LEFT, 0, 1)
+    grads.step(RIGHT, 1, 0)
+    grads.step(LEFT, 2, 0)
     mixed.finish(0)
     mixed.finish(1)
-    grads.step(RIGHT, 1, 1)
-    grads.step(LEFT, 0, 1)
     grads.step(RIGHT, 2, 0)
     grads.step(LEFT, 3, 0)
     grads.step(RIGHT, 2, 1)

time: 128 us -> 118 us (0.922)
  Pallas kernels: 126 us -> 116 us
    pallas_call x1, Pallas kernels: 126 us -> 116 us  [local(): pl.pallas_call(layer_kernel, out_shape=jax.ShapeDtypeStruct((rows, 2 * HA...]
where the time goes in v4:
time: 118 us
  Pallas kernels  116 us (98%)
  local copies, waits for them, and re-layouts  1.85 us (2%)
    pallas_call x1, Pallas kernels, local(): pl.pallas_call(layer_kernel, out_shape=jax.ShapeDtypeStruct((rows, 2 * HA...  116 us

profile of v4, /device:TPU:64, one launch (start us, length us, event | category | flops | bytes accessed | tf_op | source)
XLA Modules:
  0.0 118.0 jit_solution(5393986273484066924)
XLA Ops:
  0.6 115.5 %shard_map.77 = bf16[512,512]{1,0:T(8,128)(2,1)} custom-call(bf16[512,256]{1,0:T(8,128)(2,1)} %hid.1, bf16[2048,1280]{1,0:T(8,128)(2,1)} %pw.1, bf16[4,2048]{1,0:T(4,128)(2,1)} %bitcast.2, f32[2,128]{1,0:T(2,128)} %bitcast.3, bf16[256,2048]{1,0:T(8,128)(2,1)} %ow.1, bf16[512,256]{1,0:T(8,128)(2,1)} %cot.1), custom_call_target="tpu_custom_call" | custom-call | tf_op jit(solution)/shard_map/pallas_call | solution.py:633
  116.2 1.9 %fusion = (bf16[512,256]{1,0:T(8,128)(2,1)}, bf16[512,256]{1,0:T(8,128)(2,1)}) fusion(bf16[512,512]{1,0:T(8,128)(2,1)} %shard_map.77), kind=kLoop, calls=%fused_computation | loop fusion | bytes 1048576 | tf_op jit(solution)/shard_map/slice | solution.py:652

commit v5 on v4

--- a/solution.py
+++ b/solution.py
@@ -9,6 +9,7 @@
 REFL = 2
 CT = 64
 CR = CT * REFL
+PASS = 8
 BATCH = 4
 MESH = pl.DeviceIdType.MESH
 F32 = jnp.float32
@@ -242,7 +243,7 @@
     hids, cots, pw_v, ow_v, proj, logit, dn,
     q_i, k_i, w_i, uv_i, t_i, a_i, pm_i, po_i, mc_i, msave, qp_s, q2_s, o2_s,
     oc, mo, cslot, yslot_f, xslot_f, fin_f,
-    s_s, u_s, do_s, y_s, e_s, d_s, esum, ec, yslot_b, xslot_b, fin_b,
+    s_s, u_s, do_s, y_s, e_s, back_mo, esum, ec, yslot_b, xslot_b, fin_b,
     normed, gproj, glogit, msent, mcame, gsent, gcame,
     sems_h, sems_c, sems_f, sems_b, sems_m, sems_g, sems_w,
 ):
@@ -273,17 +274,13 @@
             logit[...] = part_b if i == 0 else logit[...] + part_b
 
     def chunk_batch(step, carry):
-        @pl.when(step == 1)
-        def _():
-            gather_step(cots, sems_c, z, 1, (0,))
-
         r_at, c_at = orders(CR, CR, False, False)
         below = r_at > c_at
         diff = jnp.bitwise_xor(r_at, c_at)
         tr, tc = orders(CT, CR, True, False)
         visible = tc <= 2 * tr + 1
         eye = jnp.where(r_at == c_at, 1.0, 0.0)
-        jobs = [(h, BATCH * step + cc) for cc in range(BATCH) for h in range(heads)]
+        jobs = [(h, PASS * step + cc) for cc in range(PASS) for h in range(heads)]
         ks, bs, vs, qs = [], [], [], []
         for h, c in jobs:
             a, c1, c2, v1, v2 = head_rows(proj, c, h)
@@ -320,9 +317,9 @@
             oc[h, crows(c), :] = m[:, DK:]
         return carry
 
-    lax.fori_loop(0, chunks // BATCH, chunk_batch, 0)
-
-    gather_step(cots, sems_c, z, 1, (1,))
+    lax.fori_loop(0, chunks // PASS, chunk_batch, 0)
+
+    gather_step(cots, sems_c, z, 1)
 
     for h in range(heads):
         mo[h, :, :DK] = eye_nat()
@@ -357,11 +354,7 @@
     gather_step(cots, sems_c, z, 2, (1,))
 
     def read_maps(step, carry):
-        @pl.when(step == 1)
-        def _():
-            gather_step(cots, sems_c, z, 3, (0,))
-
-        jobs = [(h, BATCH * step + cc) for cc in range(BATCH) for h in range(heads)]
+        jobs = [(h, PASS * step + cc) for cc in range(PASS) for h in range(heads)]
         sees = [lhs(a_i[h, trows(c), :]) for h, c in jobs]
         aws = [pmm(a2, rhs(w_i[h, crows(c), :])) for (h, c), a2 in zip(jobs, sees)]
         aus = [pmm(a2, rhs(uv_i[h, crows(c), :])) for (h, c), a2 in zip(jobs, sees)]
@@ -375,10 +368,10 @@
             o2_s[h, trows(c), :] = o2 + au
         return carry
 
-    lax.fori_loop(0, chunks // BATCH, read_maps, 0)
+    lax.fori_loop(0, chunks // PASS, read_maps, 0)
     for c in sends:
         c.wait()
-    gather_step(cots, sems_c, z, 3, (1,))
+    gather_step(cots, sems_c, z, 3)
     got = [yslot_f[lax.rem(y + 4 - i, 4)] for i in range(4)]
     p1 = got[0].astype(F32)
     p2 = compose(got[1], p1, mmb)
@@ -460,12 +453,7 @@
         c.start()
 
     def inner_parts(step, carry):
-        @pl.when(step == 1)
-        def _():
-            mixed.step(RIGHT, 1, 0)
-            mixed.step(LEFT, 1, 1)
-
-        jobs = [(h, BATCH * step + cc) for cc in range(BATCH) for h in range(heads)]
+        jobs = [(h, PASS * step + cc) for cc in range(PASS) for h in range(heads)]
         starts = [rhs(fin_f[h]) for h in range(heads)]
         states = [
             pmm(lhs(pm_i[h, crows(c), :]), starts[h]) + po_i[h, crows(c), :] for h, c in jobs
@@ -483,7 +471,9 @@
             e_s[h, crows(c), :] = side[CR:]
         return carry
 
-    lax.fori_loop(0, chunks // BATCH, inner_parts, 0)
+    mixed.step(RIGHT, 1, 0)
+    mixed.step(LEFT, 1, 1)
+    lax.fori_loop(0, chunks // PASS, inner_parts, 0)
     mixed.step(RIGHT, 2, 1)
     mixed.step(LEFT, 2, 0)
     for c in sends:
@@ -500,6 +490,22 @@
     for c in sends:
         c.start()
     inside = jnp.where(y == 2, r3, jnp.where(y == 1, r2, r1))
+    for h in range(heads):
+        back_mo[h, :, :DK] = eye_nat()
+        back_mo[h, :, DK:] = jnp.zeros((DK, DK), F32)
+
+    def suffix(step, carry):
+        c = chunks - 1 - step
+        for h in range(heads):
+            cur = back_mo[h]
+            pm_i[h, crows(c), :] = cur[:, :DK]
+            po_i[h, crows(c), :] = cur[:, DK:]
+            r = mmt(mc_i[h, crows(c), :], cur)
+            back_mo[h, :, :DK] = r[:, :DK]
+            back_mo[h, :, DK:] = r[:, DK:] + e_s[h, crows(c), :]
+        return carry
+
+    lax.fori_loop(0, chunks, suffix, 0)
     m_x = [xslot_f[lax.rem(x + 4 - i, 4), :, :DK].T for i in (1, 2)]
     mixed.step(RIGHT, 2, 0)
     mixed.step(LEFT, 2, 1)
@@ -520,16 +526,6 @@
     mixed.step(LEFT, 3, 0)
     c1.wait()
 
-    def chain(step, carry):
-        c = chunks - 1 - step
-        for h in range(heads):
-            cur = fin_b[h]
-            d_s[h, crows(c), :] = cur
-            fin_b[h] = mmt(mc_i[h, crows(c), :], cur) + e_s[h, crows(c), :]
-        return carry
-
-    lax.fori_loop(0, chunks, chain, 0)
-
     def grad_term(dest, j):
         rows = slice(j * HALF, (j + 1) * HALF)
         part = pl.ds(pl.multiple_of(dest * HALF, HALF), HALF)
@@ -554,7 +550,8 @@
         jobs = [(h, BATCH * step + cc) for cc in range(BATCH) for h in range(heads)]
         ks = [k_i[h, crows(c), :] for h, c in jobs]
         k4 = [rhs(k) for k in ks]
-        ds = [d_s[h, crows(c), :] for h, c in jobs]
+        ends = [rhs(fin_b[h]) for h in range(heads)]
+        ds = [pmm(lhs(pm_i[h, crows(c), :]), ends[h]) + po_i[h, crows(c), :] for h, c in jobs]
         us = [u_s[h, crows(c), :] for h, c in jobs]
         dus = [mm(k, d) + y_s[h, crows(c), :] for (h, c), k, d in zip(jobs, ks, ds)]
         zs = [mmt(t_i[h, crows(c), :], du) for (h, c), du in zip(jobs, dus)]
@@ -640,7 +637,7 @@
             buf(rows, proj_weight.shape[1]), buf(rows, 4), buf(rows, 2 * DK),
             part, full, full, full, full, part, full, full, full, low(4, DK, DK), part, part, part,
             full, wide, wide, low(4, DK, 2 * DK), low(4, DK, 2 * DK), buf(3, DK, DK),
-            full, full, part, full, full, full, square, square, low(4, DK, DK), low(4, DK, DK), buf(3, DK, DK),
+            full, full, part, full, full, wide, square, square, low(4, DK, DK), low(4, DK, DK), buf(3, DK, DK),
             low(rows, 2 * DK), low(rows, 10 * DK), low(rows, 4),
             low(2, 4, rows, HALF), low(2, 4, rows, HALF),
             low(2, 4, rows, HALF), low(2, 4, rows, HALF),

time: 118 us -> 115 us (0.975)
  Pallas kernels: 116 us -> 112 us
    pallas_call x1, Pallas kernels: 116 us -> 112 us  [local(): pl.pallas_call(layer_kernel, out_shape=jax.ShapeDtypeStruct((rows, 2 * HA...]
where the time goes in v5:
time: 115 us
  Pallas kernels  112 us (97%)
  local copies, waits for them, and re-layouts  1.85 us (2%)
    pallas_call x1, Pallas kernels, local(): pl.pallas_call(layer_kernel, out_shape=jax.ShapeDtypeStruct((rows, 2 * HA...  112 us

profile of v5, /device:TPU:64, one launch (start us, length us, event | category | flops | bytes accessed | tf_op | source)
XLA Modules:
  0.0 114.8 jit_solution(9843869417064370034)
XLA Ops:
  0.6 112.3 %shard_map.77 = bf16[512,512]{1,0:T(8,128)(2,1)} custom-call(bf16[512,256]{1,0:T(8,128)(2,1)} %hid.1, bf16[2048,1280]{1,0:T(8,128)(2,1)} %pw.1, bf16[4,2048]{1,0:T(4,128)(2,1)} %bitcast.2, f32[2,128]{1,0:T(2,128)} %bitcast.3, bf16[256,2048]{1,0:T(8,128)(2,1)} %ow.1, bf16[512,256]{1,0:T(8,128)(2,1)} %cot.1), custom_call_target="tpu_custom_call" | custom-call | tf_op jit(solution)/shard_map/pallas_call | solution.py:630
  113.0 1.9 %fusion = (bf16[512,256]{1,0:T(8,128)(2,1)}, bf16[512,256]{1,0:T(8,128)(2,1)}) fusion(bf16[512,512]{1,0:T(8,128)(2,1)} %shard_map.77), kind=kLoop, calls=%fused_computation | loop fusion | bytes 1048576 | tf_op jit(solution)/shard_map/slice | solution.py:649

commit v6 on v5

--- a/solution.py
+++ b/solution.py
@@ -119,6 +119,7 @@
 
 RIGHT, LEFT = 0, 1
 HALF = 256
+PIECE = 128
 
 
 def beside(z, way):
@@ -127,7 +128,7 @@
 
 def gather_unit(buf, sems, z, way, d, j):
     src, dst = (d - 1, d) if way == RIGHT else ((9 - d) % 8, 8 - d)
-    rows = pl.ds(j * HALF, HALF)
+    rows = pl.ds(j * PIECE, PIECE)
     return pltpu.make_async_remote_copy(
         src_ref=buf.at[src, rows],
         dst_ref=buf.at[dst, rows],
@@ -139,17 +140,17 @@
 
 
 def gather_has(way, d, j):
-    return d < 4 or (d == 4 and j == way)
+    return d < 4 or (d == 4 and j // 2 == way)
 
 
 def gather_start(buf, sems, z):
-    for j in (0, 1):
+    for j in range(4):
         for way in (RIGHT, LEFT):
             gather_unit(buf, sems, z, way, 1, j).start()
 
 
 def gather_step(buf, sems, z, d, halves=(0, 1)):
-    for j in halves:
+    for j in [2 * half + i for half in halves for i in (0, 1)]:
         for way in (RIGHT, LEFT):
             if gather_has(way, d, j):
                 gather_unit(buf, sems, z, way, d, j).wait_recv()
@@ -159,7 +160,7 @@
 
 def gather_end(buf, sems, z):
     for d in (1, 2, 3, 4):
-        for j in (0, 1):
+        for j in range(4):
             for way in (RIGHT, LEFT):
                 if gather_has(way, d, j):
                     gather_unit(buf, sems, z, way, d, j).wait_send()
@@ -171,7 +172,7 @@
         self.sent, self.came, self.sems = sent, came, sems
 
     def unit(self, way, s, j):
-        rows = pl.ds(j * HALF, HALF)
+        rows = pl.ds(j * PIECE, PIECE)
         return pltpu.make_async_remote_copy(
             src_ref=self.sent.at[way, s, rows],
             dst_ref=self.came.at[way, s, rows],
@@ -187,29 +188,35 @@
     def step(self, way, s, j):
         if not self.has(way, s, j):
             return
-        rows = slice(j * HALF, (j + 1) * HALF)
         dest = lax.rem(self.z + ((4 - s) if way == RIGHT else (4 + s)), 8)
-        term = self.own(dest, j)
-        if s > 0 and self.has(way, s - 1, j):
-            self.unit(way, s - 1, j).wait_recv()
-            term = term + self.came[way, s - 1, rows].astype(F32)
-        self.sent[way, s, rows] = term.astype(BF16)
-        self.unit(way, s, j).start()
+        terms = self.own(dest, j)
+        for i in (0, 1):
+            p = 2 * j + i
+            rows = slice(p * PIECE, (p + 1) * PIECE)
+            term = terms[i * PIECE : (i + 1) * PIECE]
+            if s > 0 and self.has(way, s - 1, j):
+                self.unit(way, s - 1, p).wait_recv()
+                term = term + self.came[way, s - 1, rows].astype(F32)
+            self.sent[way, s, rows] = term.astype(BF16)
+            self.unit(way, s, p).start()
 
     def finish(self, j):
-        rows = slice(j * HALF, (j + 1) * HALF)
-        term = self.own(self.z, j)
-        for way in (RIGHT, LEFT):
-            self.unit(way, 3, j).wait_recv()
-            term = term + self.came[way, 3, rows].astype(F32)
-        self.out[rows, self.col : self.col + HALF] = term.astype(BF16)
+        terms = self.own(self.z, j)
+        for i in (0, 1):
+            p = 2 * j + i
+            rows = slice(p * PIECE, (p + 1) * PIECE)
+            term = terms[i * PIECE : (i + 1) * PIECE]
+            for way in (RIGHT, LEFT):
+                self.unit(way, 3, p).wait_recv()
+                term = term + self.came[way, 3, rows].astype(F32)
+            self.out[rows, self.col : self.col + HALF] = term.astype(BF16)
 
     def end(self):
         for way in (RIGHT, LEFT):
             for s in range(4):
-                for j in (0, 1):
-                    if self.has(way, s, j):
-                        self.unit(way, s, j).wait_send()
+                for p in range(4):
+                    if self.has(way, s, p // 2):
+                        self.unit(way, s, p).wait_send()
 
 
 def send(src, dst, sems, i, seq):
@@ -375,14 +382,15 @@
     got = [yslot_f[lax.rem(y + 4 - i, 4)] for i in range(4)]
     p1 = got[0].astype(F32)
     p2 = compose(got[1], p1, mmb)
-    p3 = compose(got[2], p2, mmb)
-    xslot_f[0] = compose(got[3], p3, mmb).astype(BF16)
+    upper = compose(got[3], got[2].astype(F32), mmb)
+    xslot_f[0] = compose(upper, p2).astype(BF16)
     sends = [
         send(xslot_f.at[0], xslot_f.at[d], sems_f, 3 + d, at(lax.rem(x + d, 4), y, core))
         for d in (1, 2, 3)
     ]
     for c in sends:
         c.start()
+    p3 = compose(got[2], p2, mmb)
     before = jnp.where(y == 1, p1, jnp.where(y == 2, p2, p3))
     m_y = [g[:, :DK].T for g in got]
     suf1 = mmb(m_y[2], m_y[3].astype(F32))
@@ -641,8 +649,8 @@
             low(rows, 2 * DK), low(rows, 10 * DK), low(rows, 4),
             low(2, 4, rows, HALF), low(2, 4, rows, HALF),
             low(2, 4, rows, HALF), low(2, 4, rows, HALF),
-            dma(2, 2, 4, 2), dma(2, 2, 4, 2), dma(2, 8), dma(2, 8),
-            dma(2, 2, 4, 2), dma(2, 2, 4, 2), dma(2),
+            dma(2, 2, 4, 4), dma(2, 2, 4, 4), dma(2, 8), dma(2, 8),
+            dma(2, 2, 4, 4), dma(2, 2, 4, 4), dma(2),
         ],
         compiler_params=params(1, 60),
     )(hidden_in, proj_weight, beta_weight.T, norm_gain.reshape(2, DK), out_weight, cotangent)

time: 115 us -> 112 us (0.974)
  Pallas kernels: 112 us -> 109 us
    pallas_call x1, Pallas kernels: 112 us -> 109 us  [local(): pl.pallas_call(layer_kernel, out_shape=jax.ShapeDtypeStruct((rows, 2 * HA...]
where the time goes in v6:
time: 112 us; the launch traced here: 111 us
  Pallas kernels  109 us (97%)
  local copies, waits for them, and re-layouts  1.85 us (2%)
    pallas_call x1, Pallas kernels, local(): pl.pallas_call(layer_kernel, out_shape=jax.ShapeDtypeStruct((rows, 2 * HA...  109 us

profile of v6, /device:TPU:64, one launch (start us, length us, event | category | flops | bytes accessed | tf_op | source)
XLA Modules:
  0.0 111.1 jit_solution(2588900816355105641)
XLA Ops:
  0.6 108.6 %shard_map.77 = bf16[512,512]{1,0:T(8,128)(2,1)} custom-call(bf16[512,256]{1,0:T(8,128)(2,1)} %hid.1, bf16[2048,1280]{1,0:T(8,128)(2,1)} %pw.1, bf16[4,2048]{1,0:T(4,128)(2,1)} %bitcast.2, f32[2,128]{1,0:T(2,128)} %bitcast.3, bf16[256,2048]{1,0:T(8,128)(2,1)} %ow.1, bf16[512,256]{1,0:T(8,128)(2,1)} %cot.1), custom_call_target="tpu_custom_call" | custom-call | tf_op jit(solution)/shard_map/pallas_call | solution.py:638
  109.2 1.9 %fusion = (bf16[512,256]{1,0:T(8,128)(2,1)}, bf16[512,256]{1,0:T(8,128)(2,1)}) fusion(bf16[512,512]{1,0:T(8,128)(2,1)} %shard_map.77), kind=kLoop, calls=%fused_computation | loop fusion | bytes 1048576 | tf_op jit(solution)/shard_map/slice | solution.py:657
